TPU v7x, 256 devices: a whole 4x4x8 slice. The times are simulated.
256 devices in a mesh: attn: 16 (over x, y_lo, core), ffn: 8 (over z), tp: 2 (over y_hi).
Axes of the slice: x: 4, y: 4 (y_hi: 2, y_lo: 2; y = y_hi * 2 + y_lo), z: 8, core: 2. Of those that a mesh axis runs over, the one named last changes fastest.
Arguments:
- queries: bfloat16 [2, 64, 16384], P(None, 'attn', ('ffn', 'tp')), may hold values from -20 to 20
- new_pairs: bfloat16 [2, 64, 512], P(None, 'attn'), may hold values from -5 to 5
- kv_pool: bfloat16 [1024, 64, 512], P('attn'), may hold values from -5 to 5
- table_first: int32 [64, 16], P('attn'), may hold values from 0 to 47
- table_second: int32 [64, 16], P('attn'), may hold values from 0 to 63
- lengths: int32 [2, 64], P(None, 'attn'), may hold values from 1 to 1024, 32768 in all within a row
- migrations: int32 [16, 16], P('attn'), may hold values from 0 to 47
- residual: bfloat16 [2, 64, 7168], P(None, None, 'attn'), may hold values from -50 to 50
- out_proj: bfloat16 [16384, 7168], P(('ffn', 'tp'), 'attn'), may hold values from -0.75 to 0.75
- norm_gain: bfloat16 [7168], P('attn'), may hold values from 0.25 to 1.75
- router: bfloat16 [7168, 8], P('attn', 'ffn'), may hold values from -0.0625 to 0.0625
- routes: int32 [2, 64, 3], replicated, may hold values from 0 to 7, all different within a row; in each aligned block of 64 rows (0 to 63, 64 to 127, ..., all dimensions but the last counted through in order) at most 48 rows name the same one
- gate_weight: bfloat16 [8, 7168, 5120], P('ffn', 'attn', 'tp'), may hold values from -0.0625 to 0.0625
- up_weight: bfloat16 [8, 7168, 5120], P('ffn', 'attn', 'tp'), may hold values from -0.0625 to 0.0625
- down_weight: bfloat16 [8, 5120, 7168], P('ffn', 'tp', 'attn'), may hold values from -0.078125 to 0.078125
Outputs:
- mixed: bfloat16 [2, 64, 7168], P(None, ('ffn', 'tp'), 'attn')
Inputs may be any that keep to these rules, and one draw needn't show every extreme that they name: `table_first`: local pages of the row's own attention device. `table_second`: local pages of the row's own attention device. `lengths`: the largest length is reached in each step. `migrations`: local pages of the sending device. `routes`: each row names 3 different experts; in each step no expert is named by more than 48 rows, a bound that some block reaches.
All inputs are finite; a program needn't handle non-finite values. No bound on the sum of `lengths` on one device may be relied on, other than what follows from the above.
Results may differ from a plain program's by a relative error of at most 0.023.
Values may be sent and summed in bfloat16 or wider, within the bound.
A program may use at most 64 MiB of HBM per device.

v0:
```python
import jax
import jax.numpy as jnp
from jax import lax
from jax.sharding import PartitionSpec as P

D = 7168


EPSILON = 1e-06


def attend(queries, page_pool, page_table, new_pair, lengths, head_size):
    row_count, slot_count = page_table.shape
    tokens = slot_count * page_pool.shape[1]
    gathered = jnp.take(page_pool, page_table.reshape(-1), axis=0).reshape(
        row_count, tokens, 2 * head_size
    )
    query = queries.reshape(row_count, -1, head_size)
    factor = head_size ** (-0.5)
    scores = (
        jnp.einsum(
            "rhd,rtd->rht", query, gathered[:, :, :head_size], preferred_element_type=jnp.float32
        )
        * factor
    )
    own_score = (
        jnp.einsum(
            "rhd,rd->rh", query, new_pair[:, :head_size], preferred_element_type=jnp.float32
        )[:, :, None]
        * factor
    )
    place = jnp.arange(tokens, dtype=jnp.int32)
    scores = jnp.where((place[None, :] < lengths[:, None])[:, None, :], scores, -jnp.inf)
    highest = jnp.maximum(jnp.max(scores, axis=2, keepdims=True), own_score)
    weights = jnp.exp(scores - highest)
    own_weight = jnp.exp(own_score - highest)
    denominator = jnp.sum(weights, axis=2) + own_weight[:, :, 0]
    mixed = jnp.einsum(
        "rht,rtd->rhd",
        weights.astype(jnp.bfloat16),
        gathered[:, :, head_size:],
        preferred_element_type=jnp.float32,
    )
    rounded = lax.optimization_barrier(own_weight.astype(jnp.bfloat16)).astype(jnp.float32)
    mixed = mixed + rounded * new_pair[:, None, head_size:].astype(jnp.float32)
    return (mixed / denominator[:, :, None]).astype(jnp.bfloat16).reshape(row_count, -1)


def slot_rows(picks, experts, capacity):
    row_count = picks.shape[0]
    labels = jnp.arange(experts, dtype=jnp.int32)
    chosen = jnp.any(picks[:, :, None] == labels[None, None, :], axis=1)
    ranking = jnp.cumsum(chosen.astype(jnp.int32), axis=0) - 1
    target = jnp.where(chosen, ranking, capacity)
    owner = jnp.broadcast_to(labels[None, :], (row_count, experts))
    source = jnp.broadcast_to(jnp.arange(row_count, dtype=jnp.int32)[:, None], (row_count, experts))
    return jnp.full((experts, capacity), -1, jnp.int32).at[owner, target].set(source, mode="drop")


def on_device(
    queries,
    new_pairs,
    kv_pool,
    table_first,
    table_second,
    lengths,
    migrations,
    residual,
    out_proj,
    norm_gain,
    router,
    routes,
    gate_weight,
    up_weight,
    down_weight,
):
    head_size = new_pairs.shape[-1] // 2
    groups = lax.axis_size("ffn") * lax.axis_size("tp")
    experts = router.shape[1] * lax.axis_size("ffn")
    row_total = routes.shape[1]
    capacity = min(row_total, 2 * row_total * routes.shape[2] // experts)
    page_count = kv_pool.shape[0]
    incoming = migrations.shape[1]
    expert = lax.axis_index("ffn")
    position = lax.axis_index(("ffn", "tp"))
    outgoing = jnp.take(kv_pool, migrations[0], axis=0)
    arrived = lax.all_to_all(outgoing, "attn", split_axis=0, concat_axis=0, tiled=True)
    new_pool = jnp.concatenate([kv_pool[: page_count - incoming], arrived], axis=0)
    gain = norm_gain.astype(jnp.float32)
    outputs = []
    for step_index in range(2):
        page_pool = kv_pool if step_index == 0 else new_pool
        page_table = table_first if step_index == 0 else table_second
        attended = attend(
            queries[step_index],
            page_pool,
            page_table,
            new_pairs[step_index],
            lengths[step_index],
            head_size,
        )
        partial_value = jnp.dot(
            lax.all_gather(attended, "attn", axis=0, tiled=True),
            out_proj,
            preferred_element_type=jnp.float32,
        )
        slot_table = slot_rows(routes[step_index], experts, capacity)
        own_slots = lax.dynamic_index_in_dim(slot_table, expert, 0, keepdims=False)
        filled = (own_slots >= 0)[:, None]
        slot_index = jnp.maximum(own_slots, 0)
        wanted = jnp.repeat(slot_table, groups // experts, axis=0).reshape(-1)
        taken = jnp.take(partial_value, jnp.maximum(wanted, 0), axis=0)
        summed = lax.psum_scatter(
            jnp.where(wanted[:, None] >= 0, taken, 0.0).astype(jnp.bfloat16),
            ("ffn", "tp"),
            scatter_dimension=0,
            tiled=True,
        ).astype(jnp.float32)
        resid_rows = residual[step_index]
        hidden_rows = jnp.where(
            filled, summed + jnp.take(resid_rows, slot_index, axis=0).astype(jnp.float32), 0.0
        )
        scaled = (hidden_rows * gain).astype(jnp.bfloat16)
        gate_part = jnp.dot(scaled, gate_weight[0], preferred_element_type=jnp.float32)
        up_part = jnp.dot(scaled, up_weight[0], preferred_element_type=jnp.float32)
        square_part = jnp.sum(hidden_rows * hidden_rows, axis=1)
        logit_part = jnp.dot(scaled, router, preferred_element_type=jnp.float32)[:, 0]
        gate, up, squares, logit = (
            lax.psum(gate_part.astype(jnp.bfloat16), "attn").astype(jnp.float32),
            lax.psum(up_part.astype(jnp.bfloat16), "attn").astype(jnp.float32),
            lax.psum(square_part.astype(jnp.bfloat16), "attn").astype(jnp.float32),
            lax.psum(logit_part.astype(jnp.bfloat16), "attn").astype(jnp.float32),
        )
        inverse = lax.rsqrt(squares / D + EPSILON)
        activated = (jax.nn.silu(gate * inverse[:, None]) * (up * inverse[:, None])).astype(
            jnp.bfloat16
        )
        expert_out = jnp.dot(activated, down_weight[0], preferred_element_type=jnp.float32)
        route_weight = jax.nn.sigmoid(logit * inverse)
        added = (
            jnp.zeros_like(partial_value)
            .at[slot_index]
            .add(jnp.where(filled, route_weight[:, None] * expert_out, 0.0))
        )
        returned = lax.psum_scatter(
            (partial_value + added).astype(jnp.bfloat16),
            ("ffn", "tp"),
            scatter_dimension=0,
            tiled=True,
        ).astype(jnp.float32)
        row_share = returned.shape[0]
        own_rows = lax.dynamic_slice_in_dim(resid_rows, position * row_share, row_share, 0)
        outputs.append((own_rows.astype(jnp.float32) + returned).astype(jnp.bfloat16))
    return jnp.stack(outputs)


def solution(mesh):
    return jax.shard_map(
        on_device,
        mesh=mesh,
        in_specs=(
            P(None, "attn", ("ffn", "tp")),
            P(None, "attn", None),
            P("attn", None, None),
            P("attn", None),
            P("attn", None),
            P(None, "attn"),
            P("attn", None),
            P(None, None, "attn"),
            P(("ffn", "tp"), "attn"),
            P("attn"),
            P("attn", "ffn"),
            P(),
            P("ffn", "attn", "tp"),
            P("ffn", "attn", "tp"),
            P("ffn", "tp", "attn"),
        ),
        out_specs=P(None, ("ffn", "tp"), "attn"),
        check_vma=False,
    )
```

profile of v0, /device:TPU:1, one launch (start us, length us, event | category | flops | bytes accessed | tf_op | source)
XLA Modules:
  0.0 775.8 jit_solution(15536096175809584423)
XLA Ops:
  6.5 0.8 fusion.101
  7.3 0.7 compare_and_fusion.6
  8.0 2.8 gather_fusion
  10.8 1.2 broadcast_select_fusion.2
  12.1 7.3 all-to-all-start
  19.7 0.2 copy.31
  19.9 0.2 copy.30
  20.1 1.2 fusion.76
  21.4 22.1 %scatter_fusion = s32[8,48]{1,0:T(8,128)S(1)} fusion(s32[8,48]{1,0:T(8,128)S(1)} %broadcast.248.clone.1, s32[512]{0:T(512)S(1)} %reshape.349, s32[512]{0:T(512)S(1)} %reshape.351), kind=kCustom, calls=%fused_computation.7 | custom fusion | bytes 10240 | tf_op jit(solution)/shard_map/scatter | solution.py:57
  43.7 4.9 gather_fusion.1
  48.7 2.6 broadcast_select_fusion.1
  51.3 0.1 fusion.99
  51.5 0.7 fusion.110
  52.2 0.2 fusion.83
  52.4 0.4 fusion.63
  52.9 20.3 %all-gather = bf16[16,4,1024]{2,1,0:T(4,128)(2,1)S(1)} all-gather(bf16[1,4,1024]{2,1,0:T(4,128)(2,1)S(1)} %reshape.385), channel_id=1, replica_groups=mesh['attn'=16,'ffn'=8,'tp'=2] {'attn'}, dimensions={0}, use_global_device_ids=true | all-gather | bytes 139264 | tf_op jit(solution)/shard_map/all_gather | solution.py:103
  73.2 0.7 reshape.386
  74.0 1.3 fusion.111
  75.3 3.0 gather_fusion.2
  78.2 2.3 fusion.17
  80.6 3.9 slice.68
  84.6 0.2 copy.33
  84.8 0.9 copy.32
  85.6 2.1 fusion.78
  87.7 0.1 reshape.363
  87.8 22.1 %scatter_fusion.2 = s32[8,48]{1,0:T(8,128)S(1)} fusion(s32[8,48]{1,0:T(8,128)S(1)} %broadcast.248.clone, s32[512]{0:T(512)S(1)} %reshape.363, s32[512]{0:T(512)S(1)} %reshape.351), kind=kCustom, calls=%fused_computation.9 | custom fusion | bytes 10240 | tf_op jit(solution)/shard_map/scatter | solution.py:57
  110.4 0.1 fusion.97
  110.5 4.5 pad_maximum_fusion
  115.0 5.0 gather_fusion.4
  120.0 2.6 broadcast_select_fusion
  122.6 0.7 fusion.109
  123.4 0.2 fusion.85
  123.6 0.4 fusion.60
  124.0 16.6 %all-gather.1 = bf16[16,4,1024]{2,1,0:T(4,128)(2,1)S(1)} all-gather(bf16[1,4,1024]{2,1,0:T(4,128)(2,1)S(1)} %reshape.387), channel_id=1, replica_groups=mesh['attn'=16,'ffn'=8,'tp'=2] {'attn'}, dimensions={0}, use_global_device_ids=true | all-gather | bytes 139264 | tf_op jit(solution)/shard_map/all_gather | solution.py:103
  140.7 0.7 reshape.388
  141.3 1.3 fusion.112
  142.7 2.1 gather_fusion.5
  144.8 1.2 fusion.16
  146.0 0.2 all-reduce.10.cloned.1.call-start
  146.3 0.7 gather_fusion.6
  147.0 0.7 gather_fusion.3
  147.7 129.7 %reduce-scatter.3.cloned.1.call-done = bf16[48,448]{1,0:T(8,128)(2,1)} async-done(((bf16[768,448]{1,0:T(8,128)(2,1)}), bf16[48,448]{1,0:T(8,128)(2,1)}) %reduce-scatter.3.cloned.1.call-update) | async-done | bytes 43024 | tf_op jit(solution)/shard_map/reduce_scatter | solution.py:113
  277.4 1.1 multiply_reduce_fusion.1
  278.6 1.2 convolution_convert_fusion.2
  279.8 1.2 convolution_convert_fusion.3
  281.0 201.3 %reduce-scatter.5.cloned.1.call-done = bf16[48,448]{1,0:T(8,128)(2,1)} async-done(((bf16[768,448]{1,0:T(8,128)(2,1)}), bf16[48,448]{1,0:T(8,128)(2,1)}) %reduce-scatter.5.cloned.1.call-update) | async-done | bytes 43024 | tf_op jit(solution)/shard_map/reduce_scatter | solution.py:113
  482.3 1.1 multiply_reduce_fusion
  483.5 1.2 convolution_convert_fusion
  484.7 1.2 convolution_convert_fusion.1
  486.0 0.1 fusion.66
  486.1 0.1 fusion.67
  486.2 32.5 %all-reduce.3 = (bf16[48]{0:T(256)(128)(2,1)S(1)}, bf16[48]{0:T(256)(128)(2,1)S(1)}, bf16[48]{0:T(256)(128)(2,1)S(1)}, bf16[48]{0:T(256)(128)(2,1)S(1)}) all-reduce(bf16[48]{0:T(256)(128)(2,1)S(1)} %get-tuple-element.28, bf16[48]{0:T(256)(128)(2,1)S(1)} %fusion.67, ...), channel_id=1, replica_groups=mesh['attn'=16,'ffn'=8,'tp'=2] {'attn'}, use_global_device_ids=true, to_apply=%region_21.25 | all-reduce | flops 192 | bytes 768 | tf_op jit(solution)/shard_map/psum | solution.py:131
  518.8 92.3 %all-reduce.10.cloned.1.call-done = (bf16[48,2560]{1,0:T(8,128)(2,1)}, bf16[48,2560]{1,0:T(8,128)(2,1)}, bf16[48,2560]{1,0:T(8,128)(2,1)}, bf16[48,2560]{1,0:T(8,128)(2,1)}) async-done(((bf16[48,2560]{1,0:T(8,128)(2,1)}, bf16[48,2560]{1,0:T(8,128)(2,1)}, bf16[48,2560]{1,0:T(8,128)(2,1)}, bf16[48,2560]{1,0:T(8,128)(2,1)}), (bf16[48,2560]{1,0:T(8,128)(2,1)}, bf16[48,2560]{1,0:T(8,128)(2,1)}, ...) | async-done | bytes 983056 | tf_op jit(solution)/shard_map/psum | solution.py:130
  611.1 2.7 fusion.24
  613.8 1.0 scatter_fusion.3
  614.8 0.6 convert_element_type.207
  615.4 2.4 fusion.27
  617.9 1.0 scatter_fusion.1
  618.8 0.6 convert_element_type.183
  619.5 0.6 dynamic-slice.2
  620.7 146.5 %all-reduce.8.cloned.1.call-done = (bf16[64,448]{1,0:T(8,128)(2,1)}, bf16[64,448]{1,0:T(8,128)(2,1)}) async-done(((bf16[64,448]{1,0:T(8,128)(2,1)}, bf16[64,448]{1,0:T(8,128)(2,1)}), (bf16[64,448]{1,0:T(8,128)(2,1)}, bf16[64,448]{1,0:T(8,128)(2,1)})) %all-reduce.8.cloned.1.call-update) | async-done | bytes 114704
  767.2 0.7 fusion.96
  767.9 0.7 fusion.95
  768.6 0.6 pad_maximum_fusion.1
  (105 shorter events, 1.5 us)
Async XLA Ops:
  6.5 272.0 %copy-start = (bf16[1,448,2560]{2,1,0:T(8,128)(2,1)S(1)}, bf16[1,448,2560]{2,1,0:T(8,128)(2,1)}, u32[]{:S(2)}) copy-start(bf16[1,448,2560]{2,1,0:T(8,128)(2,1)} %param.34) | copy-start | bytes 6881284
  10.8 8.6 %copy-start.8 = (s32[4,16]{1,0:T(4,128)S(1)}, s32[4,16]{1,0:T(4,128)}, u32[]{:S(2)}) copy-start(s32[4,16]{1,0:T(4,128)} %param.24) | copy-start | bytes 772
  10.8 8.7 %copy-start.7 = (s32[2,64,3]{1,0,2:T(2,128)S(1)}, s32[2,64,3]{1,0,2:T(2,128)}, u32[]{:S(2)}) copy-start(s32[2,64,3]{1,0,2:T(2,128)} %param.32) | copy-start | bytes 4612
  12.1 98.4 %all-to-all-start = ((bf16[16,64,512]{2,1,0:T(8,128)(2,1)}), bf16[16,64,512]{2,1,0:T(8,128)(2,1)}, u32[]{:S(2)}, u32[]{:S(2)}) async-start(bf16[16,64,512]{2,1,0:T(8,128)(2,1)} %broadcast_select_fusion.2), calls=%async_computation.1 | async-start | bytes 2097152 | tf_op jit(solution)/shard_map/all_to_all | solution.py:87
  19.4 258.0 %reduce-scatter.3.cloned.1.call-start = ((), (), s32[]{:S(2)}) async-start(), calls=%async_computation.3 | async-start | bytes 835584 | tf_op jit(solution)/shard_map/reduce_scatter | solution.py:113
  21.3 22.2 %copy-start.5 = (bf16[2,4,1024]{2,1,0:T(4,128)(2,1)S(1)}, bf16[2,4,1024]{2,1,0:T(4,128)(2,1)}, u32[]{:S(2)}) copy-start(bf16[2,4,1024]{2,1,0:T(4,128)(2,1)} %param.21) | copy-start | bytes 49156
  21.4 22.3 %copy-start.11 = (s32[2,4]{1,0:T(2,128)S(1)}, s32[2,4]{1,0:T(2,128)}, u32[]{:S(2)}) copy-start(s32[2,4]{1,0:T(2,128)} %param.26) | copy-start | bytes 100
  21.4 22.3 %copy-start.6 = (bf16[2,4,512]{2,1,0:T(4,128)(2,1)S(1)}, bf16[2,4,512]{2,1,0:T(4,128)(2,1)}, u32[]{:S(2)}) copy-start(bf16[2,4,512]{2,1,0:T(4,128)(2,1)} %param.22) | copy-start | bytes 24580
  51.5 22.5 %copy-start.3 = (bf16[1024,448]{0,1:T(8,128)(2,1)S(1)}, bf16[1024,448]{0,1:T(8,128)(2,1)}, u32[]{:S(2)}) copy-start(bf16[1024,448]{0,1:T(8,128)(2,1)} %param.29) | copy-start | bytes 2752516
  80.6 401.7 %reduce-scatter.5.cloned.1.call-start = ((), (), s32[]{:S(2)}) async-start(), calls=%async_computation.4 | async-start | bytes 835584 | tf_op jit(solution)/shard_map/reduce_scatter | solution.py:113
  87.8 22.1 %copy-start.9 = (s32[4,16]{1,0:T(4,128)S(1)}, s32[4,16]{1,0:T(4,128)}, u32[]{:S(2)}) copy-start(s32[4,16]{1,0:T(4,128)} %param.25) | copy-start | bytes 772
  144.8 1.4 copy-start.10
  144.8 1.5 copy-start.4
  146.0 465.1 %all-reduce.10.cloned.1.call-start = ((), (), s32[]{:S(2)}) async-start(), calls=%async_computation.6 | async-start | bytes 1966080 | tf_op jit(solution)/shard_map/psum | solution.py:130
  277.4 2.4 copy-start.1
  482.3 2.4 copy-start.2
  484.7 1.3 copy-start.14
  485.9 281.3 %all-reduce.8.cloned.1.call-start = ((), (), s32[]{:S(2)}) async-start(), calls=%async_computation.5 | async-start | bytes 262144
  611.1 4.3 copy-start.12
  611.1 4.3 copy-start.13
  615.4 4.1 copy-start.15
Sparse Core Ops, SparseCore 0:
  80.7 196.6 reduce-scatter.2
  281.7 200.5 reduce-scatter.4
  486.0 124.9 all-reduce.9
  619.6 147.5 all-reduce.7
where the time goes:
time: 786 us; the launch traced here: 776 us
  waiting for transfers between devices  570 us (73%)
  local copies, waits for them, and re-layouts  71.5 us (9%)
  blocking collectives  69.4 us (9%)
  other arithmetic  27.5 us (3%)
  matrix products  15.5 us (2%)
  between operations  14.4 us (2%)
    reduce_scatter x2, waiting for transfers between devices, on_device(): lax.psum_scatter(jnp.where(wanted[:, None] >= 0, taken, 0.0).astype(jnp.b...  331 us
    unnamed x5, waiting for transfers between devices  147 us
    psum x1, waiting for transfers between devices, on_device(): lax.psum(up_part.astype(jnp.bfloat16), 'attn').astype(jnp.float32)  92.3 us
    scatter x2, local copies, waits for them, and re-layouts, slot_rows(): jnp.full((experts, capacity), -1, jnp.int32).at[owner, target]  44.1 us
    all_gather x2, blocking collectives, on_device(): lax.all_gather(attended, 'attn', axis=0, tiled=True)  36.9 us
    psum x1, blocking collectives, on_device(): lax.psum(square_part.astype(jnp.bfloat16), 'attn').astype(jnp.float32)  32.5 us
  transfers between devices with their start and end apart: 5, of which 4 were waited for; matrix products, arithmetic and copies ran while one was open for 12% of the time, Pallas kernels for 0%

commit v1 on v0

v1 whole, which is shorter than its diff:
```python
import jax
import jax.numpy as jnp
from jax import lax
from jax.experimental import pallas as pl
from jax.experimental.pallas import tpu as pltpu
from jax.sharding import PartitionSpec as P

F32, BF16 = jnp.float32, jnp.bfloat16
MESH = pl.DeviceIdType.MESH
D = 7168
EPSILON = 1e-6
NA, NG = 16, 16
CHIPS = 8
LOCAL = 48
PAGE, HD = 64, 256
TOKENS = LOCAL * PAGE
CHUNK = 512
CAP = 48
W = 448
NONE = -1e30
SCALE = HD ** -0.5
NT_DIMS = (((1,), (1,)), ((), ()))
QUERY, PARTIAL, HEADS_OUT, PROJ, ROWS_IN, STATS, SIBLING, REDUCE, ACT, FORWARD, BACK = range(11)


def iota(shape, axis):
    return lax.broadcasted_iota(jnp.int32, shape, axis)


def dot(a, b):
    return jnp.dot(a, b, preferred_element_type=F32)


def dot_nt(a, b):
    return lax.dot_general(a, b, NT_DIMS, preferred_element_type=F32)


def fold(block):
    return jnp.concatenate([block[..., :256], block[..., 256:]], axis=-2)


def unfold(block):
    return jnp.concatenate([block[..., :8, :], block[..., 8:, :]], axis=-1)


def silu(v):
    return v / (1.0 + jnp.exp(-v))


def body(
    queries, new_pairs, kv_pool, table_first, table_second, lengths_in, migrations_in, residual,
    out_proj, norm_gain, router, routes, gate_weight, up_weight, down_weight,
    out,
    lengths, migrations, q_v, pair_v, pool, tab1, tab2, resid_v, wo, gain_v, router_v, routes_v, wg, wu, wd,
    load_sem, send, recv,
    tx1, rx1, tx2, rx2, tx3, rx3, tx4, rx4, tx5, rx5, tx6, rx6, txs, rxs, tx7, rx7, tx8, rx8, tx9, rx9,
    score, hidden_v, slots_v, rows_v, pick, spread, edge, own_v,
):
    me = lax.axis_index("attn")
    expert = lax.axis_index("ffn")
    g_me = expert * 2 + lax.axis_index("tp")
    core = lax.rem(me, 2)
    chip = me // 2
    sibling = me + 1 - 2 * core

    pairs = [
        (queries, q_v), (table_second, tab2), (table_first, tab1), (new_pairs, pair_v),
        (lengths_in, lengths), (migrations_in, migrations),
        (kv_pool.at[pl.ds(0, LOCAL)], pool), (routes, routes_v), (router, router_v), (norm_gain, gain_v),
        (residual, resid_v), (out_proj, wo), (gate_weight.at[0], wg), (up_weight.at[0], wu), (down_weight, wd),
    ]
    loads = [pltpu.make_async_copy(src, dst, load_sem.at[i]) for i, (src, dst) in enumerate(pairs)]
    for load in loads:
        load.start()
    (l_q, l_t2, l_t1, l_pair, l_len, l_mig, l_pool, l_routes, l_router, l_gain, l_resid, l_wo, l_wg, l_wu, l_wd) = loads

    def attn_id(i):
        return {"attn": i}

    def group_id(g):
        return {"ffn": g // 2, "tp": lax.rem(g, 2)}

    barrier = pltpu.get_barrier_semaphore()

    def greet(i, _):
        pl.semaphore_signal(barrier, inc=1, device_id=attn_id(lax.rem(me + i, NA)), device_id_type=MESH)
        pl.semaphore_signal(barrier, inc=1, device_id=group_id(lax.rem(g_me + i, NG)), device_id_type=MESH)
        return 0

    lax.fori_loop(1, NA, greet, 0)

    def remote(phase, src, dst, slot_to, slot_from, device):
        return pltpu.make_async_remote_copy(
            src_ref=src, dst_ref=dst, send_sem=send.at[phase, slot_to], recv_sem=recv.at[phase, slot_from],
            device_id=device, device_id_type=MESH,
        )

    l_q.wait()
    l_t2.wait()
    l_len.wait()
    q8 = jnp.concatenate([q_v[0].astype(F32), q_v[1].astype(F32)], axis=0)
    t2 = tab2[...]
    t2x = jnp.concatenate([t2, t2, t2, t2], axis=0)

    def column(rows, values):
        at = iota((rows, 1), 0)
        result = jnp.zeros((rows, 1), jnp.int32)
        for i in range(rows):
            result = jnp.where(at == i, values[i], result)
        return result

    len2 = column(16, [lengths[1, i % 4] for i in range(16)])
    len8 = column(8, [lengths[i // 4, i % 4] for i in range(8)])

    def counts(table, length, first, width):
        lane = iota((table.shape[0], width), 1)
        page, place = first + lane // PAGE, lane % PAGE
        total = jnp.zeros((table.shape[0], width), F32)
        for k in range(16):
            left = length - k * PAGE
            total = total + jnp.where((page == table[:, k:k + 1]) & (place < left), 1.0, 0.0)
        return total

    q2 = jnp.concatenate([q8[4:8, h * HD:(h + 1) * HD] for h in range(4)], axis=0).astype(BF16)
    for s in range(0, NA, 2):
        c = counts(t2x, len2, LOCAL + s, 2 * PAGE)
        tx1[s, :, 0:HD] = q2
        tx1[s, :, HD:384] = c.astype(BF16)
        tx1[s + 1, :, 0:HD] = q2
        tx1[s + 1, :, HD:384] = pltpu.roll(c, PAGE, axis=1).astype(BF16)
    rx1[me] = tx1[me]

    pl.semaphore_wait(barrier, 2 * (NA - 1))

    def spread_attn(phase, src_of, dst, slot):
        def one(i, _):
            peer = lax.rem(me + i, NA)
            remote(phase, src_of(peer), dst.at[slot], peer, slot, attn_id(peer)).start()
            return 0
        lax.fori_loop(1, NA, one, 0)

    def spread_group(phase, src_of, dst):
        def one(i, _):
            peer = lax.rem(g_me + i, NG)
            remote(phase, src_of(peer), dst.at[g_me], peer, g_me, group_id(peer)).start()
            return 0
        lax.fori_loop(1, NG, one, 0)

    def await_all(phase, src_of, dst, mine):
        def one(i, _):
            peer = lax.rem(mine + i, 16)
            remote(phase, src_of(peer), dst.at[peer], peer, peer, attn_id(me)).wait_recv()
            return 0
        lax.fori_loop(1, 16, one, 0)

    spread_attn(QUERY, lambda peer: tx1.at[peer], rx1, me)

    l_routes.wait()
    l_router.wait()
    named = [routes_v[i] == expert for i in range(3)]
    chosen = jnp.where(named[0] | named[1] | named[2], 1.0, 0.0)
    chosen = jnp.concatenate([chosen[0:1], chosen[1:2]], axis=1)
    row, lane = iota((128, 128), 0), iota((128, 128), 1)
    row_step = (row % 8) // 4
    natural = row_step * 64 + (row // 8) * 4 + row % 4
    chosen_at = jnp.sum(jnp.where(lane == natural, chosen, 0.0), axis=1, keepdims=True)
    before = (lane < natural) & (lane // 64 == row_step)
    rank = jnp.sum(jnp.where(before, chosen, 0.0), axis=1, keepdims=True).astype(jnp.int32)
    slot_at = rank + jnp.where(row_step == core, 0, CAP)
    picked = jnp.where((lane == slot_at) & (chosen_at > 0.5), 1.0, 0.0)
    spread[...] = picked.astype(BF16)
    pick[...] = jnp.transpose(picked)
    router_row = jnp.concatenate([router_v[...].astype(F32), jnp.zeros((1, 512 - W), F32)], axis=1)
    edge_row, edge_lane = iota((8, 512), 0), iota((8, 512), 1)
    edge[...] = jnp.where(
        edge_row == 0, router_row, jnp.where((edge_row == 1) & (edge_lane >= W) & (edge_lane < W + 2), 1.0, 0.0)
    ).astype(BF16)

    l_pool.wait()
    l_mig.wait()

    def serve(i, _):
        source = lax.rem(me + i, NA)

        @pl.when(i > 0)
        def _():
            remote(QUERY, tx1.at[source], rx1.at[source], source, source, attn_id(me)).wait_recv()

        page = migrations[0, source]
        count = rx1[source, :, HD:HD + PAGE].astype(F32)
        live = count > 0.5
        s = dot_nt(rx1[source, :, 0:HD], pool[page, :, 0:HD]) * SCALE
        top = jnp.max(jnp.where(live, s, NONE), axis=1, keepdims=True).astype(BF16).astype(F32)
        weight = jnp.where(live, count * jnp.exp(s - top), 0.0)
        total = jnp.sum(weight, axis=1, keepdims=True)
        high = total.astype(BF16).astype(F32)
        o = dot(weight.astype(BF16), pool[page, :, HD:2 * HD])
        at = iota((16, 128), 1)
        stat = jnp.where(at == 0, top, jnp.where(at == 1, high, jnp.where(at == 2, total - high, 0.0)))
        tx2[source, :, 0:HD] = o.astype(BF16)
        tx2[source, :, HD:384] = stat.astype(BF16)

        @pl.when(i > 0)
        def _():
            remote(PARTIAL, tx2.at[source], rx2.at[me], source, me, attn_id(source)).start()

        return 0

    lax.fori_loop(0, NA, serve, 0)
    rx2[me] = tx2[me]

    l_t1.wait()
    l_pair.wait()
    t8 = jnp.concatenate([tab1[...], t2], axis=0)
    q32 = jnp.concatenate([q8[:, h * HD:(h + 1) * HD] for h in range(4)], axis=0)
    q32b = q32.astype(BF16)
    pair8 = jnp.concatenate([pair_v[0].astype(F32), pair_v[1].astype(F32)], axis=0)
    peak = jnp.full((32, 128), NONE, F32)
    all_counts = []
    for c in range(TOKENS // CHUNK):
        pages = CHUNK // PAGE
        count = counts(t8, len8, c * pages, CHUNK)
        count = jnp.concatenate([count] * 4, axis=0)
        s = dot_nt(q32b, pool[c * pages:(c + 1) * pages, :, 0:HD].reshape(CHUNK, HD)) * SCALE
        s = jnp.where(count > 0.5, s, NONE)
        score[0, :, c * CHUNK:(c + 1) * CHUNK] = s
        score[1, :, c * CHUNK:(c + 1) * CHUNK] = count
        for b in range(CHUNK // 128):
            peak = jnp.maximum(peak, s[:, b * 128:(b + 1) * 128])
    m_local = jnp.max(peak, axis=1, keepdims=True)
    sums = jnp.zeros((32, 128), F32)
    o_local = jnp.zeros((32, HD), F32)
    for c in range(TOKENS // CHUNK):
        count = score[1, :, c * CHUNK:(c + 1) * CHUNK]
        weight = jnp.where(count > 0.5, count * jnp.exp(score[0, :, c * CHUNK:(c + 1) * CHUNK] - m_local), 0.0)
        for b in range(CHUNK // 128):
            sums = sums + weight[:, b * 128:(b + 1) * 128]
        pages = CHUNK // PAGE
        o_local = o_local + dot(
            weight.astype(BF16), pool[c * pages:(c + 1) * pages, :, HD:2 * HD].reshape(CHUNK, HD)
        )
    l_local = jnp.sum(sums, axis=1, keepdims=True)
    key32 = jnp.concatenate([pair8[:, 0:HD]] * 4, axis=0)
    value32 = jnp.concatenate([pair8[:, HD:2 * HD]] * 4, axis=0)
    own_score = jnp.sum(q32 * key32, axis=1, keepdims=True) * SCALE

    await_all(PARTIAL, lambda peer: tx2.at[peer], rx2, me)
    back = rx2[...].astype(F32)
    m_s = back[:, :, HD:HD + 1]
    l_s = back[:, :, HD + 1:HD + 2] + back[:, :, HD + 2:HD + 3]
    m_r = jnp.max(m_s, axis=0)
    w_s = jnp.exp(m_s - m_r[None])
    l_r = jnp.sum(w_s * l_s, axis=0)
    o_r = jnp.sum(w_s * back[:, :, 0:HD], axis=0)
    at = iota((16, 128), 1)
    far = jnp.concatenate([o_r, jnp.where(at == 0, m_r, l_r)], axis=1)
    nothing = jnp.where(iota((4, 384), 1) == HD, NONE, 0.0)
    far = jnp.concatenate([x for h in range(4) for x in (nothing, far[4 * h:4 * h + 4])], axis=0)
    o_r, m_r, l_r = far[:, 0:HD], far[:, HD:HD + 1], far[:, HD + 1:HD + 2]
    top = jnp.maximum(jnp.maximum(m_local, m_r), own_score)
    f_local, f_far, f_own = jnp.exp(m_local - top), jnp.exp(m_r - top), jnp.exp(own_score - top)
    below = f_local * l_local + f_far * l_r + f_own
    above = f_local * o_local + f_far * o_r + f_own.astype(BF16).astype(F32) * value32
    attended = above / below
    attended = jnp.concatenate([attended[0:16], attended[16:32]], axis=1).astype(BF16)
    tx3[...] = attended
    rx3[me] = attended
    spread_attn(HEADS_OUT, lambda peer: tx3, rx3, me)
    l_wo.wait()
    await_all(HEADS_OUT, lambda peer: tx3, rx3, me)

    gathered = rx3[...].astype(F32)
    x = [gathered[:, 8 * i:8 * i + 8, :].reshape(128, 512).astype(BF16) for i in range(2)]
    partial = jnp.zeros((128, W), F32)
    for h in range(4):
        partial = partial + dot_nt(x[h % 2][:, (h // 2) * HD:(h // 2 + 1) * HD], wo[:, h * HD:(h + 1) * HD])

    def padded(rows):
        return jnp.concatenate([rows, jnp.zeros((rows.shape[0], 512 - W), F32)], axis=1)

    tx4[...] = fold(padded(partial).reshape(NG, 8, 512)).astype(BF16)
    rx4[g_me] = tx4[g_me]
    spread_group(PROJ, lambda peer: tx4.at[peer], rx4)

    l_resid.wait()
    l_gain.wait()
    owned = iota((8, 128), 0)
    owned = (owned // 4) * 64 + g_me * 4 + owned % 4 == iota((8, 128), 1)
    own_resid = padded(dot(jnp.where(owned, 1.0, 0.0).astype(BF16), resid_v[...].reshape(128, W)))
    gain = padded(gain_v[...].astype(F32).reshape(1, W))
    await_all(PROJ, lambda peer: tx4.at[peer], rx4, g_me)
    hidden = own_resid + unfold(jnp.sum(rx4[...].astype(F32), axis=0))
    hidden_v[...] = hidden
    squares = jnp.sum(hidden * hidden, axis=1, keepdims=True)
    high = squares.astype(BF16).astype(F32)
    scaled = hidden * gain
    scaled = jnp.where(edge_lane == W, high, jnp.where(edge_lane == W + 1, squares - high, scaled))
    scaled = fold(scaled).astype(BF16)
    tx5[...] = scaled
    rx5[g_me] = scaled
    spread_group(ROWS_IN, lambda peer: tx5, rx5)
    await_all(ROWS_IN, lambda peer: tx5, rx5, g_me)

    rows = unfold(rx5[...].astype(F32)).reshape(128, 512).astype(BF16)
    rows_v[...] = rows
    stats = dot_nt(edge[...], rows)
    tx6[...] = stats
    rx6[me] = stats
    spread_attn(STATS, lambda peer: tx6, rx6, me)
    slots_v[...] = dot(pick[0:2 * CAP, :].astype(BF16), rows_v[:, 0:W]).astype(BF16)

    l_wg.wait()
    l_wu.wait()
    left = iota((2 * CAP, 128), 1) < 64

    for p in range(4):
        slots = slots_v[...]
        g = dot(slots, wg[:, 640 * p:640 * p + 640])
        u = dot(slots, wu[:, 640 * p:640 * p + 640])
        g2, u2 = g[:, 256:384], pltpu.roll(u[:, 256:384], 64, axis=1)
        pieces = (
            (g[:, 0:256], u[:, 0:256], jnp.where(left, g2, u2)),
            (g[:, 384:640], u[:, 384:640], jnp.where(left, u2, g2)),
        )
        for i in range(2):
            piece = jnp.concatenate(pieces[i], axis=1)
            j = 2 * p + i
            own_v[j] = piece[0:CAP]
            txs[j] = piece[CAP:2 * CAP].astype(BF16)
            remote(SIBLING, txs.at[j], rxs.at[j], j, j, attn_id(sibling)).start()

    def reduce_piece(i, _):
        j = lax.rem(chip + 1 + i, CHIPS)
        remote(SIBLING, txs.at[j], rxs.at[j], j, j, attn_id(sibling)).wait_recv()
        tx7[j] = (own_v[j] + rxs[j].astype(F32)).astype(BF16)

        @pl.when(i < CHIPS - 1)
        def _():
            remote(REDUCE, tx7.at[j], rx7.at[chip], j, chip, attn_id(2 * j + core)).start()

        return 0

    lax.fori_loop(0, CHIPS, reduce_piece, 0)
    rx7[chip] = tx7[chip]

    await_all(STATS, lambda peer: tx6, rx6, me)
    stats = jnp.sum(rx6[...], axis=0)
    inverse_row = lax.rsqrt(stats[1:2] / D + EPSILON)
    route_row = 1.0 / (1.0 + jnp.exp(-(stats[0:1] * inverse_row)))
    picked = pick[0:2 * CAP, :]
    inverse = jnp.sum(picked[0:CAP] * inverse_row, axis=1, keepdims=True)
    route = jnp.sum(picked * route_row, axis=1, keepdims=True)

    def await_piece(i, _):
        j = lax.rem(chip + i, CHIPS)
        remote(REDUCE, tx7.at[j], rx7.at[j], j, j, attn_id(me)).wait_recv()
        return 0

    lax.fori_loop(1, CHIPS, await_piece, 0)
    total = rx7[0].astype(F32)
    for j in range(1, CHIPS):
        total = total + rx7[j].astype(F32)
    total = total * inverse
    mixed = total[:, 512:640]
    half = silu(mixed) * pltpu.roll(mixed, 64, axis=1)
    right = jnp.where(iota((CAP, 128), 1) < 64, 0, 1)
    half = jnp.where(right == lax.rem(chip, 2), half, 0.0)
    activated = jnp.concatenate([silu(total[:, 0:256]) * total[:, 256:512], half], axis=1).astype(BF16)
    tx8[...] = activated
    rx8[0, chip] = activated
    remote(FORWARD, tx8, rx8.at[1, chip], chip, chip, attn_id(sibling)).start()

    def send_act(i, _):
        j = lax.rem(chip + i, CHIPS)
        remote(ACT, tx8, rx8.at[0, chip], j, chip, attn_id(2 * j + core)).start()
        return 0

    lax.fori_loop(1, CHIPS, send_act, 0)

    def forward(i, _):
        j = lax.rem(chip + i, CHIPS)
        remote(ACT, tx8, rx8.at[0, j], j, j, attn_id(me)).wait_recv()
        remote(FORWARD, rx8.at[0, j], rx8.at[1, j], j, j, attn_id(sibling)).start()
        return 0

    lax.fori_loop(1, CHIPS, forward, 0)
    l_wd.wait()

    def await_forward(i, _):
        remote(FORWARD, tx8, rx8.at[1, i], i, i, attn_id(me)).wait_recv()
        return 0

    lax.fori_loop(0, CHIPS, await_forward, 0)
    result = jnp.zeros((2 * CAP, W), F32)
    for p in range(4):
        parts = []
        for side in range(2):
            a, b = rx8[side, 2 * p], rx8[side, 2 * p + 1]
            middle = (a[:, 256:384].astype(F32) + b[:, 256:384].astype(F32)).astype(BF16)
            parts.append(jnp.concatenate([a[:, 0:256], middle, b[:, 0:256]], axis=1))
        result = result + dot_nt(jnp.concatenate(parts, axis=0), wd[:, 640 * p:640 * p + 640])
    result = (result * route).astype(BF16)
    added = dot(spread[:, 0:2 * CAP], result)
    tx9[...] = fold(padded(added).reshape(NG, 8, 512)).astype(BF16)
    rx9[g_me] = tx9[g_me]
    spread_group(BACK, lambda peer: tx9.at[peer], rx9)
    await_all(BACK, lambda peer: tx9.at[peer], rx9, g_me)
    final = hidden_v[...] + unfold(jnp.sum(rx9[...].astype(F32), axis=0))
    out[0] = final[0:4, 0:W].astype(BF16)
    out[1] = final[4:8, 0:W].astype(BF16)

    def done(i, _):
        peer = lax.rem(me + i, NA)
        for phase, src, dst in (
            (QUERY, tx1.at[peer], rx1.at[peer]), (PARTIAL, tx2.at[peer], rx2.at[peer]), (HEADS_OUT, tx3, rx3.at[peer]),
            (STATS, tx6, rx6.at[peer]),
        ):
            remote(phase, src, dst, peer, peer, attn_id(me)).wait_send()
        peer = lax.rem(g_me + i, NG)
        for phase, src, dst in (
            (PROJ, tx4.at[peer], rx4.at[peer]), (ROWS_IN, tx5, rx5.at[peer]), (BACK, tx9.at[peer], rx9.at[peer]),
        ):
            remote(phase, src, dst, peer, peer, attn_id(me)).wait_send()
        return 0

    lax.fori_loop(1, NA, done, 0)

    def done_pieces(j, _):
        remote(SIBLING, txs.at[j], rxs.at[j], j, j, attn_id(me)).wait_send()
        remote(FORWARD, tx8, rx8.at[1, j], j, j, attn_id(me)).wait_send()

        @pl.when(j != chip)
        def _():
            remote(REDUCE, tx7.at[j], rx7.at[j], j, j, attn_id(me)).wait_send()
            remote(ACT, tx8, rx8.at[0, j], j, j, attn_id(me)).wait_send()

        return 0

    lax.fori_loop(0, CHIPS, done_pieces, 0)


def on_device(
    queries, new_pairs, kv_pool, table_first, table_second, lengths, migrations, residual,
    out_proj, norm_gain, router, routes, gate_weight, up_weight, down_weight,
):
    vmem, smem = pltpu.VMEM, pltpu.SMEM
    return pl.pallas_call(
        body,
        out_shape=jax.ShapeDtypeStruct((2, 4, W), BF16),
        in_specs=[pl.BlockSpec(memory_space=pltpu.HBM)] * 15,
        out_specs=pl.BlockSpec(memory_space=pltpu.VMEM),
        scratch_shapes=[
            smem((2, 4), jnp.int32), smem((1, 16), jnp.int32),
            vmem((2, 4, 1024), BF16), vmem((2, 4, 512), BF16), vmem((LOCAL, PAGE, 2 * HD), BF16),
            vmem((4, 16), jnp.int32), vmem((4, 16), jnp.int32), vmem((2, 64, W), BF16), vmem((W, 1024), BF16),
            vmem((W,), BF16), vmem((1, W), BF16), vmem((3, 2, 64), jnp.int32),
            vmem((W, 2560), BF16), vmem((W, 2560), BF16), vmem((W, 2560), BF16),
            pltpu.SemaphoreType.DMA((15,)), pltpu.SemaphoreType.DMA((11, 16)), pltpu.SemaphoreType.DMA((11, 16)),
            vmem((NA, 16, 384), BF16), vmem((NA, 16, 384), BF16),
            vmem((NA, 16, 384), BF16), vmem((NA, 16, 384), BF16),
            vmem((16, 512), BF16), vmem((NA, 16, 512), BF16),
            vmem((NG, 16, 256), BF16), vmem((NG, 16, 256), BF16),
            vmem((16, 256), BF16), vmem((NG, 16, 256), BF16),
            vmem((8, 128), F32), vmem((NA, 8, 128), F32),
            vmem((CHIPS, CAP, 640), BF16), vmem((CHIPS, CAP, 640), BF16),
            vmem((CHIPS, CAP, 640), BF16), vmem((CHIPS, CAP, 640), BF16),
            vmem((CAP, 384), BF16), vmem((2, CHIPS, CAP, 384), BF16),
            vmem((NG, 16, 256), BF16), vmem((NG, 16, 256), BF16),
            vmem((2, 32, TOKENS), F32), vmem((8, 512), F32), vmem((2 * CAP, W), BF16), vmem((128, 512), BF16),
            vmem((128, 128), F32), vmem((128, 128), BF16), vmem((8, 512), BF16), vmem((CHIPS, CAP, 640), F32),
        ],
        compiler_params=pltpu.CompilerParams(
            collective_id=0, has_side_effects=True, vmem_limit_bytes=60 * 1024 * 1024
        ),
        name="layer",
    )(
        queries, new_pairs, kv_pool, table_first, table_second, lengths, migrations, residual,
        out_proj.T, norm_gain, router.T, routes.transpose(2, 0, 1), gate_weight, up_weight, down_weight[0].T,
    )


def solution(mesh):
    return jax.shard_map(
        on_device,
        mesh=mesh,
        in_specs=(
            P(None, "attn", ("ffn", "tp")),
            P(None, "attn", None),
            P("attn", None, None),
            P("attn", None),
            P("attn", None),
            P(None, "attn"),
            P("attn", None),
            P(None, None, "attn"),
            P(("ffn", "tp"), "attn"),
            P("attn"),
            P("attn", "ffn"),
            P(),
            P("ffn", "attn", "tp"),
            P("ffn", "attn", "tp"),
            P("ffn", "tp", "attn"),
        ),
        out_specs=P(None, ("ffn", "tp"), "attn"),
        check_vma=False,
    )
```

time: 786 us -> 74.1 us (0.09); the launches traced: 776 us -> 73.9 us
  waiting for transfers between devices: 570 us -> 0 us
  Pallas kernels: 0 us -> 72.6 us
  local copies, waits for them, and re-layouts: 71.5 us -> 1.3 us
  blocking collectives: 69.4 us -> 0 us
  other arithmetic: 27.5 us -> 0 us
  matrix products: 15.5 us -> 0 us
  between operations: 14.4 us -> 0.01 us
    reduce_scatter x2 -> x0, waiting for transfers between devices: 331 us -> none  [on_device(): lax.psum_scatter(jnp.where(wanted[:, None] >= 0, taken, 0.0).astype(jnp.b...]
    unnamed x5 -> x0, waiting for transfers between devices: 147 us -> none
    psum x1 -> x0, waiting for transfers between devices: 92.3 us -> none  [on_device(): lax.psum(up_part.astype(jnp.bfloat16), 'attn').astype(jnp.float32)]
    pallas_call x0 -> x1, Pallas kernels: none -> 72.6 us  [on_device(): pl.pallas_call(body, out_shape=jax.ShapeDtypeStruct((2, 4, W), BF16), in_...]
    scatter x2 -> x0, local copies, waits for them, and re-layouts: 44.1 us -> none  [slot_rows(): jnp.full((experts, capacity), -1, jnp.int32).at[owner, target]]
    all_gather x2 -> x0, blocking collectives: 36.9 us -> none  [on_device(): lax.all_gather(attended, 'attn', axis=0, tiled=True)]
    psum x1 -> x0, blocking collectives: 32.5 us -> none  [on_device(): lax.psum(square_part.astype(jnp.bfloat16), 'attn').astype(jnp.float32)]
    gather x7 -> x0, local copies, waits for them, and re-layouts: 19.1 us -> none  [the longest x2 9.93 us: attend(): jnp.take(page_pool, page_table.reshape(-1), axis=0)]
  transfers between devices with their start and end apart: 5 -> 0, of which waited for: 4 -> 0; matrix products, arithmetic and copies ran while one was open for 12% -> 0% of each run, Pallas kernels for 0% -> 0%
where the time goes in v1:
time: 74.1 us; the launch traced here: 73.9 us
  Pallas kernels  72.6 us (98%)
  local copies, waits for them, and re-layouts  1.3 us (2%)
    pallas_call x1, Pallas kernels, on_device(): pl.pallas_call(body, out_shape=jax.ShapeDtypeStruct((2, 4, W), BF16), in_...  72.6 us

profile of v1, /device:TPU:1, one launch (start us, length us, event | category | flops | bytes accessed | tf_op | source)
XLA Modules:
  0.0 73.9 jit_solution(10611384988071370016)
XLA Ops:
  0.0 72.6 %layer.1 = bf16[2,4,448]{2,1,0:T(4,128)(2,1)} custom-call(bf16[2,4,1024]{2,1,0:T(4,128)(2,1)} %queries.1, bf16[2,4,512]{2,1,0:T(4,128)(2,1)} %new_pairs.1, bf16[64,64,512]{2,1,0:T(8,128)(2,1)} %kv_pool.1, s32[4,16]{1,0:T(4,128)} %table_first.1, s32[4,16]{1,0:T(4,128)} %table_second.1, s32[2,4]{1,0:T(2,128)} %lengths_in.1, s32[1,16]{1,0:T(1,128)} %migrations_in.1, ...), custom_call_target="tpu_custom_call" | custom-call | tf_op jit(solution)/shard_map/layer/pallas_call | solution.py:447
  72.6 1.3 %copy.17 = bf16[2,4,448]{2,1,0:T(4,128)(2,1)} copy(bf16[2,4,448]{2,1,0:T(4,128)(2,1)} %layer.1) | data formatting | bytes 14336

commit v2 on v1

--- a/solution.py
+++ b/solution.py
@@ -20,7 +20,12 @@
 NONE = -1e30
 SCALE = HD ** -0.5
 NT_DIMS = (((1,), (1,)), ((), ()))
+ATTN_ORDER = [(dx, dy, dc) for dx in (2, 1, 3, 0) for dy in (1, 0) for dc in (0, 1) if (dx, dy, dc) != (0, 0, 0)]
+GROUP_ORDER = [(dz, dt) for dz in (4, 3, 5, 2, 6, 1, 7, 0) for dt in (1, 0) if (dz, dt) != (0, 0)]
+NEIGHBOURS = [(1, 1), (7, 1), (0, 1), (1, 0), (7, 0)]
+NEAR_FIRST = (0, 1, 3, 2)
 QUERY, PARTIAL, HEADS_OUT, PROJ, ROWS_IN, STATS, SIBLING, REDUCE, ACT, FORWARD, BACK = range(11)
+TOGETHER = (PARTIAL, HEADS_OUT, PROJ, ROWS_IN, STATS, BACK)
 
 
 def iota(shape, axis):
@@ -52,9 +57,9 @@
     out_proj, norm_gain, router, routes, gate_weight, up_weight, down_weight,
     out,
     lengths, migrations, q_v, pair_v, pool, tab1, tab2, resid_v, wo, gain_v, router_v, routes_v, wg, wu, wd,
-    load_sem, send, recv,
+    load_sem, send, recv, gossip,
     tx1, rx1, tx2, rx2, tx3, rx3, tx4, rx4, tx5, rx5, tx6, rx6, txs, rxs, tx7, rx7, tx8, rx8, tx9, rx9,
-    score, hidden_v, slots_v, rows_v, pick, spread, edge, own_v,
+    score, base_v, hidden_v, slots_v, rows_v, pick, spread, edge, own_v,
 ):
     me = lax.axis_index("attn")
     expert = lax.axis_index("ffn")
@@ -62,6 +67,17 @@
     core = lax.rem(me, 2)
     chip = me // 2
     sibling = me + 1 - 2 * core
+    at_x, at_y = me // 4, lax.rem(chip, 2)
+    at_t = lax.rem(g_me, 2)
+
+    def attn_peer(dx, dy, dc):
+        return lax.rem(at_x + dx, 4) * 4 + lax.rem(at_y + dy, 2) * 2 + lax.rem(core + dc, 2)
+
+    def chip_peer(dx, dy):
+        return lax.rem(at_x + dx, 4) * 2 + lax.rem(at_y + dy, 2)
+
+    def group_peer(dz, dt):
+        return lax.rem(expert + dz, 8) * 2 + lax.rem(at_t + dt, 2)
 
     pairs = [
         (queries, q_v), (table_second, tab2), (table_first, tab1), (new_pairs, pair_v),
@@ -82,16 +98,21 @@
 
     barrier = pltpu.get_barrier_semaphore()
 
-    def greet(i, _):
-        pl.semaphore_signal(barrier, inc=1, device_id=attn_id(lax.rem(me + i, NA)), device_id_type=MESH)
-        pl.semaphore_signal(barrier, inc=1, device_id=group_id(lax.rem(g_me + i, NG)), device_id_type=MESH)
-        return 0
-
-    lax.fori_loop(1, NA, greet, 0)
+    for step in ATTN_ORDER:
+        pl.semaphore_signal(barrier, inc=1, device_id=attn_id(attn_peer(*step)), device_id_type=MESH)
+    for step in NEIGHBOURS:
+        pl.semaphore_signal(barrier, inc=1, device_id=group_id(group_peer(*step)), device_id_type=MESH)
+
+    def tell(i):
+        for dz in (1, 7):
+            pl.semaphore_signal(gossip.at[i], inc=1, device_id=group_id(group_peer(dz, 0)), device_id_type=MESH)
+
+    def hear(i):
+        pl.semaphore_wait(gossip.at[i], 2)
 
     def remote(phase, src, dst, slot_to, slot_from, device):
         return pltpu.make_async_remote_copy(
-            src_ref=src, dst_ref=dst, send_sem=send.at[phase, slot_to], recv_sem=recv.at[phase, slot_from],
+            src_ref=src, dst_ref=dst, send_sem=send.at[phase], recv_sem=recv.at[phase, 0 if phase in TOGETHER else slot_from],
             device_id=device, device_id_type=MESH,
         )
 
@@ -129,31 +150,6 @@
         tx1[s + 1, :, 0:HD] = q2
         tx1[s + 1, :, HD:384] = pltpu.roll(c, PAGE, axis=1).astype(BF16)
     rx1[me] = tx1[me]
-
-    pl.semaphore_wait(barrier, 2 * (NA - 1))
-
-    def spread_attn(phase, src_of, dst, slot):
-        def one(i, _):
-            peer = lax.rem(me + i, NA)
-            remote(phase, src_of(peer), dst.at[slot], peer, slot, attn_id(peer)).start()
-            return 0
-        lax.fori_loop(1, NA, one, 0)
-
-    def spread_group(phase, src_of, dst):
-        def one(i, _):
-            peer = lax.rem(g_me + i, NG)
-            remote(phase, src_of(peer), dst.at[g_me], peer, g_me, group_id(peer)).start()
-            return 0
-        lax.fori_loop(1, NG, one, 0)
-
-    def await_all(phase, src_of, dst, mine):
-        def one(i, _):
-            peer = lax.rem(mine + i, 16)
-            remote(phase, src_of(peer), dst.at[peer], peer, peer, attn_id(me)).wait_recv()
-            return 0
-        lax.fori_loop(1, 16, one, 0)
-
-    spread_attn(QUERY, lambda peer: tx1.at[peer], rx1, me)
 
     l_routes.wait()
     l_router.wait()
@@ -176,39 +172,37 @@
         edge_row == 0, router_row, jnp.where((edge_row == 1) & (edge_lane >= W) & (edge_lane < W + 2), 1.0, 0.0)
     ).astype(BF16)
 
+    def padded(rows):
+        return jnp.concatenate([rows, jnp.zeros((rows.shape[0], 512 - W), F32)], axis=1)
+
+    l_resid.wait()
+    l_gain.wait()
+    owned = iota((8, 128), 0)
+    owned = (owned // 4) * 64 + g_me * 4 + owned % 4 == iota((8, 128), 1)
+    base_v[0:8] = padded(dot(jnp.where(owned, 1.0, 0.0).astype(BF16), resid_v[...].reshape(128, W)))
+    base_v[8:16] = jnp.broadcast_to(padded(gain_v[...].astype(F32).reshape(1, W)), (8, 512))
+
+    pl.semaphore_wait(barrier, len(ATTN_ORDER) + len(NEIGHBOURS))
+
+    def spread_attn(phase, src_of, dst, slot):
+        for step in ATTN_ORDER:
+            peer = attn_peer(*step)
+            remote(phase, src_of(peer), dst.at[slot], peer, slot, attn_id(peer)).start()
+
+    def spread_group(phase, src_of, dst):
+        for step in GROUP_ORDER:
+            peer = group_peer(*step)
+            remote(phase, src_of(peer), dst.at[g_me], peer, g_me, group_id(peer)).start()
+
+    def await_all(phase, dst):
+        every = dst.at[pl.ds(0, 15)]
+        remote(phase, every, every, 0, 0, attn_id(me)).wait_recv()
+
+    spread_attn(QUERY, lambda peer: tx1.at[peer], rx1, me)
+    tell(0)
+
     l_pool.wait()
     l_mig.wait()
-
-    def serve(i, _):
-        source = lax.rem(me + i, NA)
-
-        @pl.when(i > 0)
-        def _():
-            remote(QUERY, tx1.at[source], rx1.at[source], source, source, attn_id(me)).wait_recv()
-
-        page = migrations[0, source]
-        count = rx1[source, :, HD:HD + PAGE].astype(F32)
-        live = count > 0.5
-        s = dot_nt(rx1[source, :, 0:HD], pool[page, :, 0:HD]) * SCALE
-        top = jnp.max(jnp.where(live, s, NONE), axis=1, keepdims=True).astype(BF16).astype(F32)
-        weight = jnp.where(live, count * jnp.exp(s - top), 0.0)
-        total = jnp.sum(weight, axis=1, keepdims=True)
-        high = total.astype(BF16).astype(F32)
-        o = dot(weight.astype(BF16), pool[page, :, HD:2 * HD])
-        at = iota((16, 128), 1)
-        stat = jnp.where(at == 0, top, jnp.where(at == 1, high, jnp.where(at == 2, total - high, 0.0)))
-        tx2[source, :, 0:HD] = o.astype(BF16)
-        tx2[source, :, HD:384] = stat.astype(BF16)
-
-        @pl.when(i > 0)
-        def _():
-            remote(PARTIAL, tx2.at[source], rx2.at[me], source, me, attn_id(source)).start()
-
-        return 0
-
-    lax.fori_loop(0, NA, serve, 0)
-    rx2[me] = tx2[me]
-
     l_t1.wait()
     l_pair.wait()
     t8 = jnp.concatenate([tab1[...], t2], axis=0)
@@ -244,7 +238,35 @@
     value32 = jnp.concatenate([pair8[:, HD:2 * HD]] * 4, axis=0)
     own_score = jnp.sum(q32 * key32, axis=1, keepdims=True) * SCALE
 
-    await_all(PARTIAL, lambda peer: tx2.at[peer], rx2, me)
+    for dx in NEAR_FIRST:
+        steps = [(dx, dy, dc) for dy in (0, 1) for dc in (0, 1)]
+        sources = [attn_peer(*step) for step in steps]
+        for step, source in zip(steps, sources):
+            if step != (0, 0, 0):
+                remote(QUERY, tx1.at[source], rx1.at[source], source, source, attn_id(me)).wait_recv()
+        pages = [migrations[0, source] for source in sources]
+        asked = [rx1[source] for source in sources]
+        count = jnp.concatenate([a[:, HD:HD + PAGE].astype(F32) for a in asked], axis=0)
+        s = jnp.concatenate([dot_nt(a[:, 0:HD], pool[page, :, 0:HD]) for a, page in zip(asked, pages)], axis=0) * SCALE
+        live = count > 0.5
+        top = jnp.max(jnp.where(live, s, NONE), axis=1, keepdims=True).astype(BF16).astype(F32)
+        weight = jnp.where(live, count * jnp.exp(s - top), 0.0)
+        total = jnp.sum(weight, axis=1, keepdims=True)
+        high = total.astype(BF16).astype(F32)
+        at = iota((64, 128), 1)
+        stat = jnp.where(at == 0, top, jnp.where(at == 1, high, jnp.where(at == 2, total - high, 0.0))).astype(BF16)
+        weight = weight.astype(BF16)
+        for i, (step, source) in enumerate(zip(steps, sources)):
+            tx2[source, :, 0:HD] = dot(weight[16 * i:16 * i + 16], pool[pages[i], :, HD:2 * HD]).astype(BF16)
+            tx2[source, :, HD:384] = stat[16 * i:16 * i + 16]
+        for step, source in zip(steps, sources):
+            if step != (0, 0, 0):
+                remote(PARTIAL, tx2.at[source], rx2.at[me], source, me, attn_id(source)).start()
+    rx2[me] = tx2[me]
+    hear(0)
+    tell(1)
+
+    await_all(PARTIAL, rx2)
     back = rx2[...].astype(F32)
     m_s = back[:, :, HD:HD + 1]
     l_s = back[:, :, HD + 1:HD + 2] + back[:, :, HD + 2:HD + 3]
@@ -266,8 +288,10 @@
     tx3[...] = attended
     rx3[me] = attended
     spread_attn(HEADS_OUT, lambda peer: tx3, rx3, me)
+    hear(1)
+    tell(2)
     l_wo.wait()
-    await_all(HEADS_OUT, lambda peer: tx3, rx3, me)
+    await_all(HEADS_OUT, rx3)
 
     gathered = rx3[...].astype(F32)
     x = [gathered[:, 8 * i:8 * i + 8, :].reshape(128, 512).astype(BF16) for i in range(2)]
@@ -275,31 +299,23 @@
     for h in range(4):
         partial = partial + dot_nt(x[h % 2][:, (h // 2) * HD:(h // 2 + 1) * HD], wo[:, h * HD:(h + 1) * HD])
 
-    def padded(rows):
-        return jnp.concatenate([rows, jnp.zeros((rows.shape[0], 512 - W), F32)], axis=1)
-
     tx4[...] = fold(padded(partial).reshape(NG, 8, 512)).astype(BF16)
     rx4[g_me] = tx4[g_me]
+    hear(2)
     spread_group(PROJ, lambda peer: tx4.at[peer], rx4)
 
-    l_resid.wait()
-    l_gain.wait()
-    owned = iota((8, 128), 0)
-    owned = (owned // 4) * 64 + g_me * 4 + owned % 4 == iota((8, 128), 1)
-    own_resid = padded(dot(jnp.where(owned, 1.0, 0.0).astype(BF16), resid_v[...].reshape(128, W)))
-    gain = padded(gain_v[...].astype(F32).reshape(1, W))
-    await_all(PROJ, lambda peer: tx4.at[peer], rx4, g_me)
-    hidden = own_resid + unfold(jnp.sum(rx4[...].astype(F32), axis=0))
+    await_all(PROJ, rx4)
+    hidden = base_v[0:8] + unfold(jnp.sum(rx4[...].astype(F32), axis=0))
     hidden_v[...] = hidden
     squares = jnp.sum(hidden * hidden, axis=1, keepdims=True)
     high = squares.astype(BF16).astype(F32)
-    scaled = hidden * gain
+    scaled = hidden * base_v[8:16]
     scaled = jnp.where(edge_lane == W, high, jnp.where(edge_lane == W + 1, squares - high, scaled))
     scaled = fold(scaled).astype(BF16)
     tx5[...] = scaled
     rx5[g_me] = scaled
     spread_group(ROWS_IN, lambda peer: tx5, rx5)
-    await_all(ROWS_IN, lambda peer: tx5, rx5, g_me)
+    await_all(ROWS_IN, rx5)
 
     rows = unfold(rx5[...].astype(F32)).reshape(128, 512).astype(BF16)
     rows_v[...] = rows
@@ -313,10 +329,10 @@
     l_wu.wait()
     left = iota((2 * CAP, 128), 1) < 64
 
-    for p in range(4):
-        slots = slots_v[...]
-        g = dot(slots, wg[:, 640 * p:640 * p + 640])
-        u = dot(slots, wu[:, 640 * p:640 * p + 640])
+    def compute_pair(p):
+        lanes = pl.ds(pl.multiple_of(640 * p, 128), 640)
+        g = dot(slots_v[...], wg[:, lanes])
+        u = dot(slots_v[...], wu[:, lanes])
         g2, u2 = g[:, 256:384], pltpu.roll(u[:, 256:384], 64, axis=1)
         pieces = (
             (g[:, 0:256], u[:, 0:256], jnp.where(left, g2, u2)),
@@ -329,21 +345,22 @@
             txs[j] = piece[CAP:2 * CAP].astype(BF16)
             remote(SIBLING, txs.at[j], rxs.at[j], j, j, attn_id(sibling)).start()
 
-    def reduce_piece(i, _):
-        j = lax.rem(chip + 1 + i, CHIPS)
-        remote(SIBLING, txs.at[j], rxs.at[j], j, j, attn_id(sibling)).wait_recv()
-        tx7[j] = (own_v[j] + rxs[j].astype(F32)).astype(BF16)
-
-        @pl.when(i < CHIPS - 1)
-        def _():
-            remote(REDUCE, tx7.at[j], rx7.at[chip], j, chip, attn_id(2 * j + core)).start()
-
-        return 0
-
-    lax.fori_loop(0, CHIPS, reduce_piece, 0)
-    rx7[chip] = tx7[chip]
-
-    await_all(STATS, lambda peer: tx6, rx6, me)
+    def reduce_pair(dx):
+        for dy in (1, 0):
+            j = chip_peer(dx, dy)
+            remote(SIBLING, txs.at[j], rxs.at[j], j, j, attn_id(sibling)).wait_recv()
+            tx7[j] = (own_v[j] + rxs[j].astype(F32)).astype(BF16)
+            if (dx, dy) != (0, 0):
+                remote(REDUCE, tx7.at[j], rx7.at[chip], j, chip, attn_id(2 * j + core)).start()
+
+    far_first = (2, 1, 3, 0)
+    for k, dx in enumerate(far_first):
+        compute_pair(lax.rem(at_x + dx, 4))
+        if k > 0:
+            reduce_pair(far_first[k - 1])
+    reduce_pair(0)
+
+    await_all(STATS, rx6)
     stats = jnp.sum(rx6[...], axis=0)
     inverse_row = lax.rsqrt(stats[1:2] / D + EPSILON)
     route_row = 1.0 / (1.0 + jnp.exp(-(stats[0:1] * inverse_row)))
@@ -351,15 +368,13 @@
     inverse = jnp.sum(picked[0:CAP] * inverse_row, axis=1, keepdims=True)
     route = jnp.sum(picked * route_row, axis=1, keepdims=True)
 
-    def await_piece(i, _):
-        j = lax.rem(chip + i, CHIPS)
-        remote(REDUCE, tx7.at[j], rx7.at[j], j, j, attn_id(me)).wait_recv()
-        return 0
-
-    lax.fori_loop(1, CHIPS, await_piece, 0)
-    total = rx7[0].astype(F32)
-    for j in range(1, CHIPS):
-        total = total + rx7[j].astype(F32)
+    total = tx7[chip].astype(F32)
+    for dx in NEAR_FIRST:
+        for dy in (0, 1):
+            if (dx, dy) != (0, 0):
+                j = chip_peer(dx, dy)
+                remote(REDUCE, tx7.at[j], rx7.at[j], j, j, attn_id(me)).wait_recv()
+                total = total + rx7[j].astype(F32)
     total = total * inverse
     mixed = total[:, 512:640]
     half = silu(mixed) * pltpu.roll(mixed, 64, axis=1)
@@ -368,75 +383,58 @@
     activated = jnp.concatenate([silu(total[:, 0:256]) * total[:, 256:512], half], axis=1).astype(BF16)
     tx8[...] = activated
     rx8[0, chip] = activated
+    for dx in far_first:
+        for dy in (1, 0):
+            if (dx, dy) != (0, 0):
+                j = chip_peer(dx, dy)
+                remote(ACT, tx8, rx8.at[0, chip], j, chip, attn_id(2 * j + core)).start()
     remote(FORWARD, tx8, rx8.at[1, chip], chip, chip, attn_id(sibling)).start()
-
-    def send_act(i, _):
-        j = lax.rem(chip + i, CHIPS)
-        remote(ACT, tx8, rx8.at[0, chip], j, chip, attn_id(2 * j + core)).start()
-        return 0
-
-    lax.fori_loop(1, CHIPS, send_act, 0)
-
-    def forward(i, _):
-        j = lax.rem(chip + i, CHIPS)
-        remote(ACT, tx8, rx8.at[0, j], j, j, attn_id(me)).wait_recv()
-        remote(FORWARD, rx8.at[0, j], rx8.at[1, j], j, j, attn_id(sibling)).start()
-        return 0
-
-    lax.fori_loop(1, CHIPS, forward, 0)
     l_wd.wait()
 
-    def await_forward(i, _):
-        remote(FORWARD, tx8, rx8.at[1, i], i, i, attn_id(me)).wait_recv()
-        return 0
-
-    lax.fori_loop(0, CHIPS, await_forward, 0)
-    result = jnp.zeros((2 * CAP, W), F32)
-    for p in range(4):
+    def forward_pair(dx):
+        for dy in (0, 1):
+            if (dx, dy) != (0, 0):
+                j = chip_peer(dx, dy)
+                remote(ACT, tx8, rx8.at[0, j], j, j, attn_id(me)).wait_recv()
+                remote(FORWARD, rx8.at[0, j], rx8.at[1, j], j, j, attn_id(sibling)).start()
+
+    def down_pair(dx):
+        p = lax.rem(at_x + dx, 4)
+        for j in (2 * p, 2 * p + 1):
+            remote(FORWARD, tx8, rx8.at[1, j], j, j, attn_id(me)).wait_recv()
         parts = []
         for side in range(2):
             a, b = rx8[side, 2 * p], rx8[side, 2 * p + 1]
             middle = (a[:, 256:384].astype(F32) + b[:, 256:384].astype(F32)).astype(BF16)
             parts.append(jnp.concatenate([a[:, 0:256], middle, b[:, 0:256]], axis=1))
-        result = result + dot_nt(jnp.concatenate(parts, axis=0), wd[:, 640 * p:640 * p + 640])
+        lanes = pl.ds(pl.multiple_of(640 * p, 128), 640)
+        return dot_nt(jnp.concatenate(parts, axis=0), wd[:, lanes])
+
+    result = jnp.zeros((2 * CAP, W), F32)
+    for k, dx in enumerate(NEAR_FIRST):
+        forward_pair(dx)
+        if k > 0:
+            result = result + down_pair(NEAR_FIRST[k - 1])
+    result = result + down_pair(NEAR_FIRST[3])
     result = (result * route).astype(BF16)
     added = dot(spread[:, 0:2 * CAP], result)
     tx9[...] = fold(padded(added).reshape(NG, 8, 512)).astype(BF16)
     rx9[g_me] = tx9[g_me]
     spread_group(BACK, lambda peer: tx9.at[peer], rx9)
-    await_all(BACK, lambda peer: tx9.at[peer], rx9, g_me)
+
+    def sent(phase, every):
+        remote(phase, every, every, 0, 0, attn_id(me)).wait_send()
+
+    for phase, dst in ((QUERY, rx1), (PARTIAL, rx2), (HEADS_OUT, rx3), (PROJ, rx4), (ROWS_IN, rx5), (STATS, rx6), (BACK, rx9)):
+        sent(phase, dst.at[pl.ds(0, 15)])
+    sent(SIBLING, txs)
+    sent(REDUCE, tx7.at[pl.ds(0, CHIPS - 1)])
+    sent(ACT, rx8.at[0, pl.ds(0, CHIPS - 1)])
+    sent(FORWARD, rx8.at[0])
+    await_all(BACK, rx9)
     final = hidden_v[...] + unfold(jnp.sum(rx9[...].astype(F32), axis=0))
     out[0] = final[0:4, 0:W].astype(BF16)
     out[1] = final[4:8, 0:W].astype(BF16)
-
-    def done(i, _):
-        peer = lax.rem(me + i, NA)
-        for phase, src, dst in (
-            (QUERY, tx1.at[peer], rx1.at[peer]), (PARTIAL, tx2.at[peer], rx2.at[peer]), (HEADS_OUT, tx3, rx3.at[peer]),
-            (STATS, tx6, rx6.at[peer]),
-        ):
-            remote(phase, src, dst, peer, peer, attn_id(me)).wait_send()
-        peer = lax.rem(g_me + i, NG)
-        for phase, src, dst in (
-            (PROJ, tx4.at[peer], rx4.at[peer]), (ROWS_IN, tx5, rx5.at[peer]), (BACK, tx9.at[peer], rx9.at[peer]),
-        ):
-            remote(phase, src, dst, peer, peer, attn_id(me)).wait_send()
-        return 0
-
-    lax.fori_loop(1, NA, done, 0)
-
-    def done_pieces(j, _):
-        remote(SIBLING, txs.at[j], rxs.at[j], j, j, attn_id(me)).wait_send()
-        remote(FORWARD, tx8, rx8.at[1, j], j, j, attn_id(me)).wait_send()
-
-        @pl.when(j != chip)
-        def _():
-            remote(REDUCE, tx7.at[j], rx7.at[j], j, j, attn_id(me)).wait_send()
-            remote(ACT, tx8, rx8.at[0, j], j, j, attn_id(me)).wait_send()
-
-        return 0
-
-    lax.fori_loop(0, CHIPS, done_pieces, 0)
 
 
 def on_device(
@@ -455,7 +453,7 @@
             vmem((4, 16), jnp.int32), vmem((4, 16), jnp.int32), vmem((2, 64, W), BF16), vmem((W, 1024), BF16),
             vmem((W,), BF16), vmem((1, W), BF16), vmem((3, 2, 64), jnp.int32),
             vmem((W, 2560), BF16), vmem((W, 2560), BF16), vmem((W, 2560), BF16),
-            pltpu.SemaphoreType.DMA((15,)), pltpu.SemaphoreType.DMA((11, 16)), pltpu.SemaphoreType.DMA((11, 16)),
+            pltpu.SemaphoreType.DMA((15,)), pltpu.SemaphoreType.DMA((11,)), pltpu.SemaphoreType.DMA((11, 16)), pltpu.SemaphoreType.REGULAR((3,)),
             vmem((NA, 16, 384), BF16), vmem((NA, 16, 384), BF16),
             vmem((NA, 16, 384), BF16), vmem((NA, 16, 384), BF16),
             vmem((16, 512), BF16), vmem((NA, 16, 512), BF16),
@@ -466,7 +464,7 @@
             vmem((CHIPS, CAP, 640), BF16), vmem((CHIPS, CAP, 640), BF16),
             vmem((CAP, 384), BF16), vmem((2, CHIPS, CAP, 384), BF16),
             vmem((NG, 16, 256), BF16), vmem((NG, 16, 256), BF16),
-            vmem((2, 32, TOKENS), F32), vmem((8, 512), F32), vmem((2 * CAP, W), BF16), vmem((128, 512), BF16),
+            vmem((2, 32, TOKENS), F32), vmem((16, 512), F32), vmem((8, 512), F32), vmem((2 * CAP, W), BF16), vmem((128, 512), BF16),
             vmem((128, 128), F32), vmem((128, 128), BF16), vmem((8, 512), BF16), vmem((CHIPS, CAP, 640), F32),
         ],
         compiler_params=pltpu.CompilerParams(

time: 74.1 us -> 66.1 us (0.89)
  Pallas kernels: 72.6 us -> 64.6 us
    pallas_call x1, Pallas kernels: 72.6 us -> 64.6 us  [on_device(): pl.pallas_call(body, out_shape=jax.ShapeDtypeStruct((2, 4, W), BF16), in_...]
where the time goes in v2:
time: 66.1 us; the launch traced here: 65.9 us
  Pallas kernels  64.6 us (98%)
  local copies, waits for them, and re-layouts  1.3 us (2%)
    pallas_call x1, Pallas kernels, on_device(): pl.pallas_call(body, out_shape=jax.ShapeDtypeStruct((2, 4, W), BF16), in_...  64.6 us

profile of v2, /device:TPU:1, one launch (start us, length us, event | category | flops | bytes accessed | tf_op | source)
XLA Modules:
  0.0 65.9 jit_solution(16157507420726262488)
XLA Ops:
  0.0 64.6 %layer.1 = bf16[2,4,448]{2,1,0:T(4,128)(2,1)} custom-call(bf16[2,4,1024]{2,1,0:T(4,128)(2,1)} %queries.1, bf16[2,4,512]{2,1,0:T(4,128)(2,1)} %new_pairs.1, bf16[64,64,512]{2,1,0:T(8,128)(2,1)} %kv_pool.1, s32[4,16]{1,0:T(4,128)} %table_first.1, s32[4,16]{1,0:T(4,128)} %table_second.1, s32[2,4]{1,0:T(2,128)} %lengths_in.1, s32[1,16]{1,0:T(1,128)} %migrations_in.1, ...), custom_call_target="tpu_custom_call" | custom-call | tf_op jit(solution)/shard_map/layer/pallas_call | solution.py:445
  64.6 1.3 %copy.17 = bf16[2,4,448]{2,1,0:T(4,128)(2,1)} copy(bf16[2,4,448]{2,1,0:T(4,128)(2,1)} %layer.1) | data formatting | bytes 14336

commit v3 on v2

--- a/solution.py
+++ b/solution.py
@@ -21,11 +21,11 @@
 SCALE = HD ** -0.5
 NT_DIMS = (((1,), (1,)), ((), ()))
 ATTN_ORDER = [(dx, dy, dc) for dx in (2, 1, 3, 0) for dy in (1, 0) for dc in (0, 1) if (dx, dy, dc) != (0, 0, 0)]
-GROUP_ORDER = [(dz, dt) for dz in (4, 3, 5, 2, 6, 1, 7, 0) for dt in (1, 0) if (dz, dt) != (0, 0)]
-NEIGHBOURS = [(1, 1), (7, 1), (0, 1), (1, 0), (7, 0)]
+GROUP_ORDER = [(dz, dt) for dt in (1, 0) for dz in (4, 3, 5, 2, 6, 1, 7, 0) if (dz, dt) != (0, 0)]
+NEIGHBOURS = [(0, 1), (1, 0), (7, 0)]
 NEAR_FIRST = (0, 1, 3, 2)
-QUERY, PARTIAL, HEADS_OUT, PROJ, ROWS_IN, STATS, SIBLING, REDUCE, ACT, FORWARD, BACK = range(11)
-TOGETHER = (PARTIAL, HEADS_OUT, PROJ, ROWS_IN, STATS, BACK)
+QUERY, PARTIAL, HEADS_OUT, PROJ, ROWS_IN, STATS, SIBLING, REDUCE, ACT, FORWARD, BACK, HEADS_FIRST = range(12)
+TOGETHER = (PARTIAL, HEADS_OUT, PROJ, ROWS_IN, STATS, BACK, HEADS_FIRST)
 
 
 def iota(shape, axis):
@@ -239,6 +239,9 @@
     own_score = jnp.sum(q32 * key32, axis=1, keepdims=True) * SCALE
 
     for dx in NEAR_FIRST:
+        if dx == 1:
+            hear(0)
+            tell(1)
         steps = [(dx, dy, dc) for dy in (0, 1) for dc in (0, 1)]
         sources = [attn_peer(*step) for step in steps]
         for step, source in zip(steps, sources):
@@ -263,8 +266,19 @@
             if step != (0, 0, 0):
                 remote(PARTIAL, tx2.at[source], rx2.at[me], source, me, attn_id(source)).start()
     rx2[me] = tx2[me]
-    hear(0)
-    tell(1)
+    hear(1)
+    tell(2)
+
+    def of_step(rows, i):
+        return jnp.concatenate([rows[8 * h + 4 * i:8 * h + 4 * i + 4] for h in range(4)], axis=0)
+
+    top = jnp.maximum(m_local, own_score)
+    f_local, f_own = jnp.exp(m_local - top), jnp.exp(own_score - top)
+    above = f_local * o_local + f_own.astype(BF16).astype(F32) * value32
+    first_step = of_step(above / (f_local * l_local + f_own), 0).astype(BF16)
+    tx3[0] = first_step
+    rx3[0, me] = first_step
+    spread_attn(HEADS_FIRST, lambda peer: tx3.at[0], rx3.at[0], me)
 
     await_all(PARTIAL, rx2)
     back = rx2[...].astype(F32)
@@ -274,34 +288,36 @@
     w_s = jnp.exp(m_s - m_r[None])
     l_r = jnp.sum(w_s * l_s, axis=0)
     o_r = jnp.sum(w_s * back[:, :, 0:HD], axis=0)
-    at = iota((16, 128), 1)
-    far = jnp.concatenate([o_r, jnp.where(at == 0, m_r, l_r)], axis=1)
-    nothing = jnp.where(iota((4, 384), 1) == HD, NONE, 0.0)
-    far = jnp.concatenate([x for h in range(4) for x in (nothing, far[4 * h:4 * h + 4])], axis=0)
-    o_r, m_r, l_r = far[:, 0:HD], far[:, HD:HD + 1], far[:, HD + 1:HD + 2]
-    top = jnp.maximum(jnp.maximum(m_local, m_r), own_score)
-    f_local, f_far, f_own = jnp.exp(m_local - top), jnp.exp(m_r - top), jnp.exp(own_score - top)
-    below = f_local * l_local + f_far * l_r + f_own
-    above = f_local * o_local + f_far * o_r + f_own.astype(BF16).astype(F32) * value32
-    attended = above / below
-    attended = jnp.concatenate([attended[0:16], attended[16:32]], axis=1).astype(BF16)
-    tx3[...] = attended
-    rx3[me] = attended
-    spread_attn(HEADS_OUT, lambda peer: tx3, rx3, me)
-    hear(1)
-    tell(2)
+    m_near, l_near, o_near = of_step(m_local, 1), of_step(l_local, 1), of_step(o_local, 1)
+    own_near = of_step(own_score, 1)
+    top = jnp.maximum(jnp.maximum(m_near, m_r), own_near)
+    f_near, f_far, f_own = jnp.exp(m_near - top), jnp.exp(m_r - top), jnp.exp(own_near - top)
+    below = f_near * l_near + f_far * l_r + f_own
+    above = f_near * o_near + f_far * o_r + f_own.astype(BF16).astype(F32) * of_step(value32, 1)
+    second_step = (above / below).astype(BF16)
+    tx3[1] = second_step
+    rx3[1, me] = second_step
+    spread_attn(HEADS_OUT, lambda peer: tx3.at[1], rx3.at[1], me)
+    hear(2)
+    tell(3)
     l_wo.wait()
-    await_all(HEADS_OUT, rx3)
-
-    gathered = rx3[...].astype(F32)
-    x = [gathered[:, 8 * i:8 * i + 8, :].reshape(128, 512).astype(BF16) for i in range(2)]
+    await_all(HEADS_FIRST, rx3.at[0])
+    await_all(HEADS_OUT, rx3.at[1])
+
+    steps = [rx3[i].astype(F32).reshape(NA, 2, 8, HD) for i in range(2)]
+    turned = [jnp.concatenate([t[:, :, 4:8], t[:, :, 0:4]], axis=2) for t in steps]
+    upper = iota((NA, 2, 8, HD), 2) < 4
+    x = [
+        jnp.where(upper, steps[0], turned[1]).astype(BF16),
+        jnp.where(upper, turned[0], steps[1]).astype(BF16),
+    ]
     partial = jnp.zeros((128, W), F32)
     for h in range(4):
-        partial = partial + dot_nt(x[h % 2][:, (h // 2) * HD:(h // 2 + 1) * HD], wo[:, h * HD:(h + 1) * HD])
+        partial = partial + dot_nt(x[h % 2][:, h // 2].reshape(128, HD), wo[:, h * HD:(h + 1) * HD])
 
     tx4[...] = fold(padded(partial).reshape(NG, 8, 512)).astype(BF16)
     rx4[g_me] = tx4[g_me]
-    hear(2)
+    hear(3)
     spread_group(PROJ, lambda peer: tx4.at[peer], rx4)
 
     await_all(PROJ, rx4)
@@ -425,7 +441,7 @@
     def sent(phase, every):
         remote(phase, every, every, 0, 0, attn_id(me)).wait_send()
 
-    for phase, dst in ((QUERY, rx1), (PARTIAL, rx2), (HEADS_OUT, rx3), (PROJ, rx4), (ROWS_IN, rx5), (STATS, rx6), (BACK, rx9)):
+    for phase, dst in ((QUERY, rx1), (PARTIAL, rx2), (HEADS_FIRST, rx3.at[0]), (HEADS_OUT, rx3.at[1]), (PROJ, rx4), (ROWS_IN, rx5), (STATS, rx6), (BACK, rx9)):
         sent(phase, dst.at[pl.ds(0, 15)])
     sent(SIBLING, txs)
     sent(REDUCE, tx7.at[pl.ds(0, CHIPS - 1)])
@@ -453,10 +469,10 @@
             vmem((4, 16), jnp.int32), vmem((4, 16), jnp.int32), vmem((2, 64, W), BF16), vmem((W, 1024), BF16),
             vmem((W,), BF16), vmem((1, W), BF16), vmem((3, 2, 64), jnp.int32),
             vmem((W, 2560), BF16), vmem((W, 2560), BF16), vmem((W, 2560), BF16),
-            pltpu.SemaphoreType.DMA((15,)), pltpu.SemaphoreType.DMA((11,)), pltpu.SemaphoreType.DMA((11, 16)), pltpu.SemaphoreType.REGULAR((3,)),
+            pltpu.SemaphoreType.DMA((15,)), pltpu.SemaphoreType.DMA((12,)), pltpu.SemaphoreType.DMA((12, 16)), pltpu.SemaphoreType.REGULAR((4,)),
             vmem((NA, 16, 384), BF16), vmem((NA, 16, 384), BF16),
             vmem((NA, 16, 384), BF16), vmem((NA, 16, 384), BF16),
-            vmem((16, 512), BF16), vmem((NA, 16, 512), BF16),
+            vmem((2, 16, HD), BF16), vmem((2, NA, 16, HD), BF16),
             vmem((NG, 16, 256), BF16), vmem((NG, 16, 256), BF16),
             vmem((16, 256), BF16), vmem((NG, 16, 256), BF16),
             vmem((8, 128), F32), vmem((NA, 8, 128), F32),

time: 66.1 us -> 65.2 us (0.986)
  Pallas kernels: 64.6 us -> 63.7 us
    pallas_call x1, Pallas kernels: 64.6 us -> 63.7 us  [on_device(): pl.pallas_call(body, out_shape=jax.ShapeDtypeStruct((2, 4, W), BF16), in_...]
where the time goes in v3:
time: 65.2 us; the launch traced here: 65 us
  Pallas kernels  63.7 us (98%)
  local copies, waits for them, and re-layouts  1.3 us (2%)
    pallas_call x1, Pallas kernels, on_device(): pl.pallas_call(body, out_shape=jax.ShapeDtypeStruct((2, 4, W), BF16), in_...  63.7 us

profile of v3, /device:TPU:1, one launch (start us, length us, event | category | flops | bytes accessed | tf_op | source)
XLA Modules:
  0.0 65.0 jit_solution(16834247272655864328)
XLA Ops:
  0.0 63.7 %layer.1 = bf16[2,4,448]{2,1,0:T(4,128)(2,1)} custom-call(bf16[2,4,1024]{2,1,0:T(4,128)(2,1)} %queries.1, bf16[2,4,512]{2,1,0:T(4,128)(2,1)} %new_pairs.1, bf16[64,64,512]{2,1,0:T(8,128)(2,1)} %kv_pool.1, s32[4,16]{1,0:T(4,128)} %table_first.1, s32[4,16]{1,0:T(4,128)} %table_second.1, s32[2,4]{1,0:T(2,128)} %lengths_in.1, s32[1,16]{1,0:T(1,128)} %migrations_in.1, ...), custom_call_target="tpu_custom_call" | custom-call | tf_op jit(solution)/shard_map/layer/pallas_call | solution.py:461
  63.7 1.3 %copy.17 = bf16[2,4,448]{2,1,0:T(4,128)(2,1)} copy(bf16[2,4,448]{2,1,0:T(4,128)(2,1)} %layer.1) | data formatting | bytes 14336

commit v4 on v3

--- a/solution.py
+++ b/solution.py
@@ -238,7 +238,7 @@
     value32 = jnp.concatenate([pair8[:, HD:2 * HD]] * 4, axis=0)
     own_score = jnp.sum(q32 * key32, axis=1, keepdims=True) * SCALE
 
-    for dx in NEAR_FIRST:
+    for dx in (2, 1, 3, 0):
         if dx == 1:
             hear(0)
             tell(1)
@@ -427,11 +427,11 @@
         return dot_nt(jnp.concatenate(parts, axis=0), wd[:, lanes])
 
     result = jnp.zeros((2 * CAP, W), F32)
-    for k, dx in enumerate(NEAR_FIRST):
+    for k, dx in enumerate(far_first):
         forward_pair(dx)
         if k > 0:
-            result = result + down_pair(NEAR_FIRST[k - 1])
-    result = result + down_pair(NEAR_FIRST[3])
+            result = result + down_pair(far_first[k - 1])
+    result = result + down_pair(0)
     result = (result * route).astype(BF16)
     added = dot(spread[:, 0:2 * CAP], result)
     tx9[...] = fold(padded(added).reshape(NG, 8, 512)).astype(BF16)

time: 65.2 us -> 64.9 us (level)
  no operation moved by 1% of the time
where the time goes in v4:
time: 64.9 us; the launch traced here: 64.7 us
  Pallas kernels  63.3 us (98%)
  local copies, waits for them, and re-layouts  1.3 us (2%)
    pallas_call x1, Pallas kernels, on_device(): pl.pallas_call(body, out_shape=jax.ShapeDtypeStruct((2, 4, W), BF16), in_...  63.3 us
    unnamed x1, local copies, waits for them, and re-layouts  1.3 us

profile of v4, /device:TPU:1, one launch (start us, length us, event | category | flops | bytes accessed | tf_op | source)
XLA Modules:
  0.0 64.7 jit_solution(3314346935237622563)
XLA Ops:
  0.0 63.3 %layer.1 = bf16[2,4,448]{2,1,0:T(4,128)(2,1)} custom-call(bf16[2,4,1024]{2,1,0:T(4,128)(2,1)} %queries.1, bf16[2,4,512]{2,1,0:T(4,128)(2,1)} %new_pairs.1, bf16[64,64,512]{2,1,0:T(8,128)(2,1)} %kv_pool.1, s32[4,16]{1,0:T(4,128)} %table_first.1, s32[4,16]{1,0:T(4,128)} %table_second.1, s32[2,4]{1,0:T(2,128)} %lengths_in.1, s32[1,16]{1,0:T(1,128)} %migrations_in.1, ...), custom_call_target="tpu_custom_call" | custom-call | tf_op jit(solution)/shard_map/layer/pallas_call | solution.py:461
  63.4 1.3 %copy.17 = bf16[2,4,448]{2,1,0:T(4,128)(2,1)} copy(bf16[2,4,448]{2,1,0:T(4,128)(2,1)} %layer.1) | data formatting | bytes 14336

commit v5 on v4

--- a/solution.py
+++ b/solution.py
@@ -24,7 +24,8 @@
 GROUP_ORDER = [(dz, dt) for dt in (1, 0) for dz in (4, 3, 5, 2, 6, 1, 7, 0) if (dz, dt) != (0, 0)]
 NEIGHBOURS = [(0, 1), (1, 0), (7, 0)]
 NEAR_FIRST = (0, 1, 3, 2)
-QUERY, PARTIAL, HEADS_OUT, PROJ, ROWS_IN, STATS, SIBLING, REDUCE, ACT, FORWARD, BACK, HEADS_FIRST = range(12)
+CHIP_ORDER = [(dx, dy) for dx in (2, 1, 3, 0) for dy in (1, 0) if (dx, dy) != (0, 0)]
+QUERY, PARTIAL, HEADS_OUT, PROJ, ROWS_IN, STATS, SIBLING, REDUCE, ACT, FORWARD, BACK, HEADS_FIRST, REDUCE_B, ACT_B, FORWARD_B = range(15)
 TOGETHER = (PARTIAL, HEADS_OUT, PROJ, ROWS_IN, STATS, BACK, HEADS_FIRST)
 
 
@@ -58,7 +59,7 @@
     out,
     lengths, migrations, q_v, pair_v, pool, tab1, tab2, resid_v, wo, gain_v, router_v, routes_v, wg, wu, wd,
     load_sem, send, recv, gossip,
-    tx1, rx1, tx2, rx2, tx3, rx3, tx4, rx4, tx5, rx5, tx6, rx6, txs, rxs, tx7, rx7, tx8, rx8, tx9, rx9,
+    tx1, rx1, tx2, rx2, tx3, rx3, tx4, rx4, tx5, rx5, tx6, rx6, txs, rxs, tx7, rx7, tx7b, rx7b, tx8, rx8, tx8b, rx8b, tx9, rx9,
     score, base_v, hidden_v, slots_v, rows_v, pick, spread, edge, own_v,
 ):
     me = lax.axis_index("attn")
@@ -351,8 +352,8 @@
         u = dot(slots_v[...], wu[:, lanes])
         g2, u2 = g[:, 256:384], pltpu.roll(u[:, 256:384], 64, axis=1)
         pieces = (
-            (g[:, 0:256], u[:, 0:256], jnp.where(left, g2, u2)),
-            (g[:, 384:640], u[:, 384:640], jnp.where(left, u2, g2)),
+            (g[:, 0:128], u[:, 0:128], jnp.where(left, g2, u2), g[:, 128:256], u[:, 128:256]),
+            (g[:, 384:512], u[:, 384:512], jnp.where(left, u2, g2), g[:, 512:640], u[:, 512:640]),
         )
         for i in range(2):
             piece = jnp.concatenate(pieces[i], axis=1)
@@ -365,7 +366,9 @@
         for dy in (1, 0):
             j = chip_peer(dx, dy)
             remote(SIBLING, txs.at[j], rxs.at[j], j, j, attn_id(sibling)).wait_recv()
-            tx7[j] = (own_v[j] + rxs[j].astype(F32)).astype(BF16)
+            both = (own_v[j] + rxs[j].astype(F32)).astype(BF16)
+            tx7[j] = both[:, 0:384]
+            tx7b[j] = both[:, 384:640]
             if (dx, dy) != (0, 0):
                 remote(REDUCE, tx7.at[j], rx7.at[chip], j, chip, attn_id(2 * j + core)).start()
 
@@ -375,6 +378,13 @@
         if k > 0:
             reduce_pair(far_first[k - 1])
     reduce_pair(0)
+
+    def to_chips(phase, src_of, dst):
+        for step in CHIP_ORDER:
+            j = chip_peer(*step)
+            remote(phase, src_of(j), dst, j, chip, attn_id(2 * j + core)).start()
+
+    to_chips(REDUCE_B, lambda j: tx7b.at[j], rx7b.at[chip])
 
     await_all(STATS, rx6)
     stats = jnp.sum(rx6[...], axis=0)
@@ -384,51 +394,59 @@
     inverse = jnp.sum(picked[0:CAP] * inverse_row, axis=1, keepdims=True)
     route = jnp.sum(picked * route_row, axis=1, keepdims=True)
 
-    total = tx7[chip].astype(F32)
-    for dx in NEAR_FIRST:
+    def summed(phase, mine, theirs):
+        total = mine[chip].astype(F32)
+        for step in reversed(CHIP_ORDER):
+            j = chip_peer(*step)
+            remote(phase, mine.at[j], theirs.at[j], j, j, attn_id(me)).wait_recv()
+            total = total + theirs[j].astype(F32)
+        return total * inverse
+
+    total = summed(REDUCE, tx7, rx7)
+    mixed = total[:, 256:384]
+    half = silu(mixed) * pltpu.roll(mixed, 64, axis=1)
+    right = jnp.where(iota((CAP, 128), 1) < 64, 0, 1)
+    half = jnp.where(right == lax.rem(chip, 2), half, 0.0)
+    activated = jnp.concatenate([silu(total[:, 0:128]) * total[:, 128:256], half], axis=1).astype(BF16)
+    tx8[...] = activated
+    rx8[0, chip] = activated
+    to_chips(ACT, lambda j: tx8, rx8.at[0, chip])
+    remote(FORWARD, tx8, rx8.at[1, chip], chip, chip, attn_id(sibling)).start()
+    total = summed(REDUCE_B, tx7b, rx7b)
+    activated = (silu(total[:, 0:128]) * total[:, 128:256]).astype(BF16)
+    tx8b[...] = activated
+    rx8b[0, chip] = activated
+    to_chips(ACT_B, lambda j: tx8b, rx8b.at[0, chip])
+    remote(FORWARD_B, tx8b, rx8b.at[1, chip], chip, chip, attn_id(sibling)).start()
+    l_wd.wait()
+
+    def forward_pair(dx, phase, onward, src, dst):
         for dy in (0, 1):
             if (dx, dy) != (0, 0):
                 j = chip_peer(dx, dy)
-                remote(REDUCE, tx7.at[j], rx7.at[j], j, j, attn_id(me)).wait_recv()
-                total = total + rx7[j].astype(F32)
-    total = total * inverse
-    mixed = total[:, 512:640]
-    half = silu(mixed) * pltpu.roll(mixed, 64, axis=1)
-    right = jnp.where(iota((CAP, 128), 1) < 64, 0, 1)
-    half = jnp.where(right == lax.rem(chip, 2), half, 0.0)
-    activated = jnp.concatenate([silu(total[:, 0:256]) * total[:, 256:512], half], axis=1).astype(BF16)
-    tx8[...] = activated
-    rx8[0, chip] = activated
-    for dx in far_first:
-        for dy in (1, 0):
-            if (dx, dy) != (0, 0):
-                j = chip_peer(dx, dy)
-                remote(ACT, tx8, rx8.at[0, chip], j, chip, attn_id(2 * j + core)).start()
-    remote(FORWARD, tx8, rx8.at[1, chip], chip, chip, attn_id(sibling)).start()
-    l_wd.wait()
-
-    def forward_pair(dx):
-        for dy in (0, 1):
-            if (dx, dy) != (0, 0):
-                j = chip_peer(dx, dy)
-                remote(ACT, tx8, rx8.at[0, j], j, j, attn_id(me)).wait_recv()
-                remote(FORWARD, rx8.at[0, j], rx8.at[1, j], j, j, attn_id(sibling)).start()
+                remote(phase, src, dst.at[0, j], j, j, attn_id(me)).wait_recv()
+                remote(onward, dst.at[0, j], dst.at[1, j], j, j, attn_id(sibling)).start()
 
     def down_pair(dx):
         p = lax.rem(at_x + dx, 4)
         for j in (2 * p, 2 * p + 1):
             remote(FORWARD, tx8, rx8.at[1, j], j, j, attn_id(me)).wait_recv()
+            remote(FORWARD_B, tx8b, rx8b.at[1, j], j, j, attn_id(me)).wait_recv()
         parts = []
         for side in range(2):
             a, b = rx8[side, 2 * p], rx8[side, 2 * p + 1]
-            middle = (a[:, 256:384].astype(F32) + b[:, 256:384].astype(F32)).astype(BF16)
-            parts.append(jnp.concatenate([a[:, 0:256], middle, b[:, 0:256]], axis=1))
+            middle = (a[:, 128:256].astype(F32) + b[:, 128:256].astype(F32)).astype(BF16)
+            parts.append(jnp.concatenate(
+                [a[:, 0:128], rx8b[side, 2 * p], middle, b[:, 0:128], rx8b[side, 2 * p + 1]], axis=1
+            ))
         lanes = pl.ds(pl.multiple_of(640 * p, 128), 640)
         return dot_nt(jnp.concatenate(parts, axis=0), wd[:, lanes])
 
     result = jnp.zeros((2 * CAP, W), F32)
+    for dx in far_first:
+        forward_pair(dx, ACT, FORWARD, tx8, rx8)
     for k, dx in enumerate(far_first):
-        forward_pair(dx)
+        forward_pair(dx, ACT_B, FORWARD_B, tx8b, rx8b)
         if k > 0:
             result = result + down_pair(far_first[k - 1])
     result = result + down_pair(0)
@@ -447,6 +465,9 @@
     sent(REDUCE, tx7.at[pl.ds(0, CHIPS - 1)])
     sent(ACT, rx8.at[0, pl.ds(0, CHIPS - 1)])
     sent(FORWARD, rx8.at[0])
+    sent(REDUCE_B, tx7b.at[pl.ds(0, CHIPS - 1)])
+    sent(ACT_B, rx8b.at[0, pl.ds(0, CHIPS - 1)])
+    sent(FORWARD_B, rx8b.at[0])
     await_all(BACK, rx9)
     final = hidden_v[...] + unfold(jnp.sum(rx9[...].astype(F32), axis=0))
     out[0] = final[0:4, 0:W].astype(BF16)
@@ -469,7 +490,7 @@
             vmem((4, 16), jnp.int32), vmem((4, 16), jnp.int32), vmem((2, 64, W), BF16), vmem((W, 1024), BF16),
             vmem((W,), BF16), vmem((1, W), BF16), vmem((3, 2, 64), jnp.int32),
             vmem((W, 2560), BF16), vmem((W, 2560), BF16), vmem((W, 2560), BF16),
-            pltpu.SemaphoreType.DMA((15,)), pltpu.SemaphoreType.DMA((12,)), pltpu.SemaphoreType.DMA((12, 16)), pltpu.SemaphoreType.REGULAR((4,)),
+            pltpu.SemaphoreType.DMA((15,)), pltpu.SemaphoreType.DMA((15,)), pltpu.SemaphoreType.DMA((15, 16)), pltpu.SemaphoreType.REGULAR((4,)),
             vmem((NA, 16, 384), BF16), vmem((NA, 16, 384), BF16),
             vmem((NA, 16, 384), BF16), vmem((NA, 16, 384), BF16),
             vmem((2, 16, HD), BF16), vmem((2, NA, 16, HD), BF16),
@@ -477,8 +498,10 @@
             vmem((16, 256), BF16), vmem((NG, 16, 256), BF16),
             vmem((8, 128), F32), vmem((NA, 8, 128), F32),
             vmem((CHIPS, CAP, 640), BF16), vmem((CHIPS, CAP, 640), BF16),
-            vmem((CHIPS, CAP, 640), BF16), vmem((CHIPS, CAP, 640), BF16),
-            vmem((CAP, 384), BF16), vmem((2, CHIPS, CAP, 384), BF16),
+            vmem((CHIPS, CAP, 384), BF16), vmem((CHIPS, CAP, 384), BF16),
+            vmem((CHIPS, CAP, 256), BF16), vmem((CHIPS, CAP, 256), BF16),
+            vmem((CAP, 256), BF16), vmem((2, CHIPS, CAP, 256), BF16),
+            vmem((CAP, 128), BF16), vmem((2, CHIPS, CAP, 128), BF16),
             vmem((NG, 16, 256), BF16), vmem((NG, 16, 256), BF16),
             vmem((2, 32, TOKENS), F32), vmem((16, 512), F32), vmem((8, 512), F32), vmem((2 * CAP, W), BF16), vmem((128, 512), BF16),
             vmem((128, 128), F32), vmem((128, 128), BF16), vmem((8, 512), BF16), vmem((CHIPS, CAP, 640), F32),

time: 64.9 us -> 64.5 us (level)
  no operation moved by 1% of the time
where the time goes in v5:
time: 64.5 us; the launch traced here: 64 us
  Pallas kernels  62.7 us (97%)
  local copies, waits for them, and re-layouts  1.3 us (2%)
    pallas_call x1, Pallas kernels, on_device(): pl.pallas_call(body, out_shape=jax.ShapeDtypeStruct((2, 4, W), BF16), in_...  62.7 us
    unnamed x1, local copies, waits for them, and re-layouts  1.3 us

profile of v5, /device:TPU:1, one launch (start us, length us, event | category | flops | bytes accessed | tf_op | source)
XLA Modules:
  0.0 64.0 jit_solution(549204678071532998)
XLA Ops:
  0.0 62.7 %layer.1 = bf16[2,4,448]{2,1,0:T(4,128)(2,1)} custom-call(bf16[2,4,1024]{2,1,0:T(4,128)(2,1)} %queries.1, bf16[2,4,512]{2,1,0:T(4,128)(2,1)} %new_pairs.1, bf16[64,64,512]{2,1,0:T(8,128)(2,1)} %kv_pool.1, s32[4,16]{1,0:T(4,128)} %table_first.1, s32[4,16]{1,0:T(4,128)} %table_second.1, s32[2,4]{1,0:T(2,128)} %lengths_in.1, s32[1,16]{1,0:T(1,128)} %migrations_in.1, ...), custom_call_target="tpu_custom_call" | custom-call | tf_op jit(solution)/shard_map/layer/pallas_call | solution.py:482
  62.7 1.3 %copy.17 = bf16[2,4,448]{2,1,0:T(4,128)(2,1)} copy(bf16[2,4,448]{2,1,0:T(4,128)(2,1)} %layer.1) | data formatting | bytes 14336

commit v6 on v5

--- a/solution.py
+++ b/solution.py
@@ -372,11 +372,19 @@
             if (dx, dy) != (0, 0):
                 remote(REDUCE, tx7.at[j], rx7.at[chip], j, chip, attn_id(2 * j + core)).start()
 
+    def send_second(dx):
+        for dy in (1, 0):
+            if (dx, dy) != (0, 0):
+                j = chip_peer(dx, dy)
+                remote(REDUCE_B, tx7b.at[j], rx7b.at[chip], j, chip, attn_id(2 * j + core)).start()
+
     far_first = (2, 1, 3, 0)
     for k, dx in enumerate(far_first):
         compute_pair(lax.rem(at_x + dx, 4))
         if k > 0:
             reduce_pair(far_first[k - 1])
+        if k > 1:
+            send_second(far_first[k - 2])
     reduce_pair(0)
 
     def to_chips(phase, src_of, dst):
@@ -384,7 +392,8 @@
             j = chip_peer(*step)
             remote(phase, src_of(j), dst, j, chip, attn_id(2 * j + core)).start()
 
-    to_chips(REDUCE_B, lambda j: tx7b.at[j], rx7b.at[chip])
+    send_second(far_first[2])
+    send_second(0)
 
     await_all(STATS, rx6)
     stats = jnp.sum(rx6[...], axis=0)

time: 64.5 us -> 64.5 us (level)
  no operation moved by 1% of the time
where the time goes in v6:
time: 64.5 us; the launch traced here: 64.1 us
  Pallas kernels  62.7 us (97%)
  local copies, waits for them, and re-layouts  1.3 us (2%)
    pallas_call x1, Pallas kernels, on_device(): pl.pallas_call(body, out_shape=jax.ShapeDtypeStruct((2, 4, W), BF16), in_...  62.7 us
    unnamed x1, local copies, waits for them, and re-layouts  1.3 us

profile of v6, /device:TPU:1, one launch (start us, length us, event | category | flops | bytes accessed | tf_op | source)
XLA Modules:
  0.0 64.1 jit_solution(3195132663511302276)
XLA Ops:
  0.0 62.7 %layer.1 = bf16[2,4,448]{2,1,0:T(4,128)(2,1)} custom-call(bf16[2,4,1024]{2,1,0:T(4,128)(2,1)} %queries.1, bf16[2,4,512]{2,1,0:T(4,128)(2,1)} %new_pairs.1, bf16[64,64,512]{2,1,0:T(8,128)(2,1)} %kv_pool.1, s32[4,16]{1,0:T(4,128)} %table_first.1, s32[4,16]{1,0:T(4,128)} %table_second.1, s32[2,4]{1,0:T(2,128)} %lengths_in.1, s32[1,16]{1,0:T(1,128)} %migrations_in.1, ...), custom_call_target="tpu_custom_call" | custom-call | tf_op jit(solution)/shard_map/layer/pallas_call | solution.py:491
  62.8 1.3 %copy.17 = bf16[2,4,448]{2,1,0:T(4,128)(2,1)} copy(bf16[2,4,448]{2,1,0:T(4,128)(2,1)} %layer.1) | data formatting | bytes 14336
